TPU v7x, 256 devices: a whole 4x4x8 slice. The times are simulated.
256 devices in a mesh: row: 16 (over x, y), col: 16 (over z, core).
Axes of the slice: x: 4, y: 4, z: 8, core: 2. Of those that a mesh axis runs over, the one named last changes fastest.
Arguments:
- stiffness: bfloat16 [36864, 36864], P('row', 'col'), may hold values from -0.046875 to 0.046875
- self_stiffness: float32 [36864], P(('row', 'col')), may hold values from 1 to 2
- stress: float32 [36864, 256], P(('row', 'col')), may hold values from -0.5 to 0.5
- state: float32 [36864, 256], P(('row', 'col')), may hold values from 0 to 1
- plate_rate: float32 [36864], P(('row', 'col')), may hold values from 0.2 to 1
- stress_gain: float32 [36864], P(('row', 'col')), may hold values from 0.5 to 2
- heal_rate: float32 [36864], P(('row', 'col')), may hold values from 0.2 to 2
- ab_ratio: float32 [36864], P(('row', 'col')), may hold values from 0.5 to 2
- step: float32 [256], replicated, may hold values from 0.05 to 0.2
Outputs:
- stress_next: float32 [36864, 256], P(('row', 'col'))
- state_next: float32 [36864, 256], P(('row', 'col'))
- error_norm: float32 [256], replicated
All inputs are finite; a program needn't handle non-finite values.
Results may differ from a plain program's by a relative error of at most 0.00085.
Values may be sent and summed in bfloat16 or wider, within the bound.
No kernel may reach another device: no remote copies, remote signals or barrier semaphores. Data moves between devices by JAX's collectives and lax.ppermute only.
A program may use at most 128 MiB of HBM per device.

v0:
```python
import jax
import jax.numpy as jnp
from jax import lax
from jax.sharding import PartitionSpec as P

tolerance = 0.01
epsilon = 1e-06


def from_root(array, axis, root):
    mine = lax.axis_index(axis) == root
    return lax.psum(jnp.where(mine, array, jnp.zeros_like(array)), axis)


def friction(stress_now, state_now, plate_vel):
    slip_rate = 2.0 * jnp.sinh(stress_now) * jnp.exp(-state_now)
    return (slip_rate, slip_rate - plate_vel[:, None])


def rates_from(state_now, slip_rate, deficit, coupled, params):
    diag_stiff, plate_vel, gain_now, heal_now, ratio_now = params
    stress_rate = gain_now[:, None] * (-diag_stiff[:, None] * deficit - coupled)
    state_rate = heal_now[:, None] * (jnp.exp(-ratio_now[:, None] * state_now) - slip_rate)
    return (stress_rate, state_rate)


def body(
    stiffness, self_stiffness, stress, state, plate_rate, stress_gain, heal_rate, ab_ratio, step
):
    owned_rows = stress.shape[0]
    row_count = lax.axis_size("row")
    col_count = lax.axis_size("col")
    row_index = lax.axis_index("row")
    col_index = lax.axis_index("col")
    patch_total = owned_rows * row_count * col_count
    source_row = col_index * row_count // col_count

    def column_block(sent_block):
        return from_root(sent_block, "row", source_row)

    params = (self_stiffness, plate_rate, stress_gain, heal_rate, ab_ratio)
    first_patch = (row_index * col_count + col_index) * owned_rows

    def coupling(sent_block):
        gathered_rows = lax.all_gather(sent_block, "col", axis=0, tiled=True)
        segment = column_block(gathered_rows)
        return lax.psum_scatter(
            jnp.dot(stiffness, segment, preferred_element_type=jnp.float32),
            "col",
            scatter_dimension=0,
            tiled=True,
        )

    def section(stress_now, state_now):
        slip_rate, deficit = friction(stress_now, state_now, params[1])
        coupled = coupling(deficit.astype(jnp.bfloat16))
        return rates_from(state_now, slip_rate, deficit, coupled, params)

    full_step = step[None, :]
    first_u, first_p = section(stress, state)
    second_u, second_p = section(stress + full_step * first_u, state + full_step * first_p)
    half_step = 0.5 * full_step
    stress_next = stress + half_step * (first_u + second_u)
    state_next = state + half_step * (first_p + second_p)
    positions = first_patch + jnp.arange(stress.shape[0], dtype=jnp.int32)
    depth = 0.5 + 1.5 * (positions.astype(jnp.float32) + 0.5) / patch_total
    squared = (depth[:, None] * half_step * (second_u - first_u)) ** 2 + (
        half_step * (second_p - first_p)
    ) ** 2
    partial_sums = jnp.sum(squared, axis=0)
    summed = lax.psum(partial_sums, ("row", "col"))
    error_norm = jnp.sqrt(summed / (2 * patch_total) + epsilon) / tolerance
    return (stress_next, state_next, error_norm)


def solution(mesh):
    return jax.shard_map(
        body,
        mesh=mesh,
        in_specs=(
            P("row", "col"),
            P(("row", "col")),
            P(("row", "col"), None),
            P(("row", "col"), None),
            P(("row", "col")),
            P(("row", "col")),
            P(("row", "col")),
            P(("row", "col")),
            P(),
        ),
        out_specs=(P(("row", "col"), None), P(("row", "col"), None), P()),
        check_vma=False,
    )
```

profile of v0, /device:TPU:1, one launch (start us, length us, event | category | flops | bytes accessed | tf_op | source)
XLA Modules:
  0.0 512.3 jit_solution(15399259939426097543)
XLA Ops:
  7.2 0.0 all-gather.3.cloned.1.call-start
  7.2 1.8 subtract_convert_fusion.1
  9.0 0.0 all-gather.3.cloned.1.call-update
  9.0 0.0 all-reduce.3.cloned.1.call-start
  9.1 44.4 %all-gather.3.cloned.1.call-done = bf16[2304,256]{1,0:T(8,128)(2,1)} async-done(((bf16[144,256]{1,0:T(8,128)(2,1)}), bf16[2304,256]{1,0:T(8,128)(2,1)}) %all-gather.3.cloned.1.call-update) | async-done | bytes 1179664 | tf_op jit(solution)/shard_map/all_gather | solution.py:45
  53.5 1.1 broadcast_select_fusion.1
  54.6 0.0 all-reduce.3.cloned.1.call-update
  54.6 0.0 reduce-scatter.7.cloned.1.call-start
  54.6 96.0 %all-reduce.3.cloned.1.call-done = bf16[2304,256]{1,0:T(8,128)(2,1)} async-done(((bf16[2304,256]{1,0:T(8,128)(2,1)}), bf16[2304,256]{1,0:T(8,128)(2,1)}) %all-reduce.3.cloned.1.call-update) | async-done | bytes 1179664 | tf_op jit(solution)/shard_map/psum | solution.py:12
  150.7 6.4 %convolution_bitcast_fusion.1 = f32[2304,256]{0,1:T(8,128)S(1)} fusion(bf16[2304,256]{1,0:T(8,128)(2,1)} %all-reduce.3.cloned.1.call-done, bf16[2304,2304]{1,0:T(8,128)(2,1)} %param.9), kind=kOutput, calls=%fused_computation.1 | convolution fusion | flops 2717908992 | bytes 14155776 | tf_op jit(solution)/shard_map/dot_general | solution.py:48
  157.0 2.0 copy.26
  159.0 0.0 copy-start.7
  159.0 0.0 copy-start.8
  159.0 0.0 copy-start.4
  159.0 0.0 copy-start
  159.0 0.0 copy-start.1
  159.0 0.0 copy-start.3
  159.0 0.0 copy-start.5
  159.0 0.0 copy-start.6
  159.1 0.0 reduce-scatter.7.cloned.1.call-update
  159.1 0.0 all-gather.5.cloned.1.call-start
  159.1 0.5 copy-done.7
  159.7 0.0 copy-done.8
  159.7 0.0 copy-done.4
  159.7 57.0 %reduce-scatter.7.cloned.1.call-done = f32[144,256]{1,0:T(8,128)} async-done(((f32[2304,256]{1,0:T(8,128)}), f32[144,256]{1,0:T(8,128)}) %reduce-scatter.7.cloned.1.call-update) | async-done | bytes 147472 | tf_op jit(solution)/shard_map/reduce_scatter | solution.py:47
  216.7 0.0 copy-done
  216.7 0.0 copy-done.1
  216.7 0.0 copy-done.3
  216.7 0.0 copy-done.5
  216.7 0.0 copy-done.6
  216.8 2.0 multiply_add_fusion
  218.7 0.7 subtract_convert_fusion
  219.4 0.0 all-gather.5.cloned.1.call-update
  219.5 0.0 all-reduce.5.cloned.1.call-start
  219.5 40.7 %all-gather.5.cloned.1.call-done = bf16[2304,256]{1,0:T(8,128)(2,1)} async-done(((bf16[144,256]{1,0:T(8,128)(2,1)}), bf16[2304,256]{1,0:T(8,128)(2,1)}) %all-gather.5.cloned.1.call-update) | async-done | bytes 1179664 | tf_op jit(solution)/shard_map/all_gather | solution.py:45
  260.2 1.1 broadcast_select_fusion
  261.3 0.0 all-reduce.5.cloned.1.call-update
  261.3 0.0 reduce-scatter.9.cloned.1.call-start
  261.4 95.9 %all-reduce.5.cloned.1.call-done = bf16[2304,256]{1,0:T(8,128)(2,1)} async-done(((bf16[2304,256]{1,0:T(8,128)(2,1)}), bf16[2304,256]{1,0:T(8,128)(2,1)}) %all-reduce.5.cloned.1.call-update) | async-done | bytes 1179664 | tf_op jit(solution)/shard_map/psum | solution.py:12
  357.2 6.4 %convolution_bitcast_fusion = f32[2304,256]{0,1:T(8,128)S(1)} fusion(bf16[2304,256]{1,0:T(8,128)(2,1)} %all-reduce.5.cloned.1.call-done, bf16[2304,2304]{1,0:T(8,128)(2,1)} %param.9), kind=kOutput, calls=%fused_computation | convolution fusion | flops 2717908992 | bytes 14155776 | tf_op jit(solution)/shard_map/dot_general | solution.py:48
  363.6 2.0 copy.28
  365.6 0.0 copy-start.2
  365.6 0.0 reduce-scatter.9.cloned.1.call-update
  365.6 57.7 %reduce-scatter.9.cloned.1.call-done = f32[144,256]{1,0:T(8,128)} async-done(((f32[2304,256]{1,0:T(8,128)}), f32[144,256]{1,0:T(8,128)}) %reduce-scatter.9.cloned.1.call-update) | async-done | bytes 147472 | tf_op jit(solution)/shard_map/reduce_scatter | solution.py:47
  423.3 0.0 copy-done.2
  423.3 1.9 add_reduce_fusion
  425.2 79.7 %psum.23 = f32[256]{0:T(256)S(1)} all-reduce(f32[256]{0:T(256)S(1)} %get-tuple-element.8), channel_id=1, replica_groups=mesh['row'=16,'col'=16] {'row','col'}, use_global_device_ids=true, to_apply=%region_5.6 | all-reduce | flops 256 | bytes 2048 | tf_op jit(solution)/shard_map/psum | solution.py:71
  504.9 0.6 sqrt_multiply_fusion
  (4 shorter events, 0.0 us)
Async XLA Ops:
  7.2 46.3 %all-gather.3.cloned.1.call-start = ((), (), s32[]{:S(2)}) async-start(), calls=%async_computation.2 | async-start | bytes 1253376 | tf_op jit(solution)/shard_map/all_gather | solution.py:45
  9.0 141.6 %all-reduce.3.cloned.1.call-start = ((), (), s32[]{:S(2)}) async-start(), calls=%async_computation.3 | async-start | bytes 2359296 | tf_op jit(solution)/shard_map/psum | solution.py:12
  54.6 162.1 %reduce-scatter.7.cloned.1.call-start = ((), (), s32[]{:S(2)}) async-start(), calls=%async_computation.6 | async-start | bytes 2506752 | tf_op jit(solution)/shard_map/reduce_scatter | solution.py:47
  159.0 0.7 copy-start.7
  159.0 0.7 copy-start.8
  159.0 0.7 copy-start.4
  159.0 57.7 %copy-start = (f32[144,256]{1,0:T(8,128)S(1)}, f32[144,256]{1,0:T(8,128)}, u32[]{:S(2)}) copy-start(f32[144,256]{1,0:T(8,128)} %param.12) | copy-start | bytes 442372
  159.0 57.7 %copy-start.1 = (f32[144,256]{1,0:T(8,128)S(1)}, f32[144,256]{1,0:T(8,128)}, u32[]{:S(2)}) copy-start(f32[144,256]{1,0:T(8,128)} %param.11) | copy-start | bytes 442372
  159.0 57.7 %copy-start.3 = (f32[144]{0:T(256)S(1)}, f32[144]{0:T(256)}, u32[]{:S(2)}) copy-start(f32[144]{0:T(256)} %param.13) | copy-start | bytes 1732
  159.0 57.7 %copy-start.5 = (f32[144]{0:T(256)S(1)}, f32[144]{0:T(256)}, u32[]{:S(2)}) copy-start(f32[144]{0:T(256)} %param.15) | copy-start | bytes 1732
  159.0 57.7 %copy-start.6 = (f32[144]{0:T(256)S(1)}, f32[144]{0:T(256)}, u32[]{:S(2)}) copy-start(f32[144]{0:T(256)} %param.14) | copy-start | bytes 1732
  159.1 101.1 %all-gather.5.cloned.1.call-start = ((), (), s32[]{:S(2)}) async-start(), calls=%async_computation.4 | async-start | bytes 1253376 | tf_op jit(solution)/shard_map/all_gather | solution.py:45
  219.5 137.8 %all-reduce.5.cloned.1.call-start = ((), (), s32[]{:S(2)}) async-start(), calls=%async_computation.5 | async-start | bytes 2359296 | tf_op jit(solution)/shard_map/psum | solution.py:12
  261.3 162.0 %reduce-scatter.9.cloned.1.call-start = ((), (), s32[]{:S(2)}) async-start(), calls=%async_computation.7 | async-start | bytes 2506752 | tf_op jit(solution)/shard_map/reduce_scatter | solution.py:47
  365.6 57.7 %copy-start.2 = (f32[144,256]{1,0:T(8,128)S(1)}, f32[144,256]{1,0:T(8,128)}, u32[]{:S(2)}) copy-start(f32[144,256]{1,0:T(8,128)} %reduce-scatter.7.cloned.1.call-done) | copy-start | bytes 442372
Sparse Core Ops, SparseCore 0:
  10.4 43.0 all-gather.2
  56.8 93.8 all-reduce.2
  159.2 57.4 reduce-scatter.6
  219.6 40.5 all-gather.4
  263.3 93.8 all-reduce.4
  365.7 57.5 reduce-scatter.8
where the time goes:
time: 513 us; the launch traced here: 512 us
  waiting for transfers between devices  392 us (76%)
  blocking collectives  79.7 us (16%)
  between operations  14.2 us (3%)
  matrix products  12.7 us (2%)
  other arithmetic  9.13 us (2%)
    psum x2, waiting for transfers between devices, from_root(): return lax.psum(jnp.where(mine, array, jnp.zeros_like(array)), axis)  192 us
    reduce_scatter x2, waiting for transfers between devices, coupling(): lax.psum_scatter(jnp.dot(stiffness, segment, preferred_element_type=jnp.f...  115 us
    all_gather x2, waiting for transfers between devices, coupling(): gathered_rows = lax.all_gather(sent_block, 'col', axis=0, tiled=True)  85.1 us
    psum x1, blocking collectives, body(): summed = lax.psum(partial_sums, ('row', 'col'))  79.7 us
    dot_general x2, matrix products, coupling(): jnp.dot(stiffness, segment, preferred_element_type=jnp.float32)  12.7 us
  transfers between devices with their start and end apart: 6, of which 6 were waited for; matrix products, arithmetic and copies ran while one was open for 0% of the time, Pallas kernels for 0%

commit v1 on v0

v1 whole, which is shorter than its diff:
```python
import jax
import jax.numpy as jnp
from jax import lax
from jax.experimental import pallas as pl
from jax.experimental.pallas import tpu as pltpu
from jax.sharding import PartitionSpec as P

tolerance = 0.01
epsilon = 1e-06
BOTH = ("row", "col")


def friction(stress_now, state_now, plate_vel):
    slip_rate = 2.0 * jnp.sinh(stress_now) * jnp.exp(-state_now)
    return (slip_rate, slip_rate - plate_vel[:, None])


def rates_from(state_now, slip_rate, deficit, coupled, params):
    diag_stiff, plate_vel, gain_now, heal_now, ratio_now = params
    stress_rate = gain_now[:, None] * (-diag_stiff[:, None] * deficit - coupled)
    state_rate = heal_now[:, None] * (jnp.exp(-ratio_now[:, None] * state_now) - slip_rate)
    return (stress_rate, state_rate)


def half_product(stiff, segment, parity, received=None):
    half, _, owned, depth = stiff.shape
    members = segment.shape[1]

    def kernel(parity_ref, stiff_ref, segment_ref, *rest):
        out_ref = rest[-1]
        rows = stiff_ref[:, parity_ref[0]].reshape(half * owned, depth)
        product = jnp.dot(rows, segment_ref[...], preferred_element_type=jnp.float32)
        product = product.reshape(half, owned, members)
        if received is not None:
            product = product + rest[0][...].astype(jnp.float32)
        out_ref[...] = product.astype(jnp.bfloat16)

    operands = (parity, stiff, segment) + (() if received is None else (received,))
    vmem = pl.BlockSpec(memory_space=pltpu.VMEM)
    return pl.pallas_call(
        kernel,
        out_shape=jax.ShapeDtypeStruct((half, owned, members), jnp.bfloat16),
        in_specs=[pl.BlockSpec(memory_space=pltpu.SMEM)] + [vmem] * (len(operands) - 1),
        out_specs=vmem,
        compiler_params=pltpu.CompilerParams(vmem_limit_bytes=32 << 20),
        cost_estimate=pl.CostEstimate(
            flops=2 * half * owned * depth * members,
            bytes_accessed=2 * half * owned * depth,
            transcendentals=0,
        ),
    )(*operands)


def body(
    stiffness, self_stiffness, stress, state, plate_rate, stress_gain, heal_rate, ab_ratio, step
):
    owned, members = stress.shape
    side = lax.axis_size("row")
    layers = side // 2
    row_index = lax.axis_index("row")
    col_index = lax.axis_index("col")
    patch_total = owned * side * side
    params = (self_stiffness, plate_rate, stress_gain, heal_rate, ab_ratio)
    first_patch = (row_index * side + col_index) * owned

    everyone = range(side)
    spread = [(a * side + b, (a ^ b) * side + a) for a in everyone for b in everyone]
    plane_groups = [[(a ^ b) * side + a for b in everyone] for a in everyone]
    same_core = [[2 * z + core for z in range(layers)] for core in range(2)]
    swap = [(c, c ^ 1) for c in everyone]
    parity = col_index % 2
    mine = parity.astype(jnp.int32).reshape(1)
    theirs = 1 - mine
    stiff = stiffness.reshape(layers, 2, owned, side * owned)

    def coupling(sent_block):
        moved = lax.ppermute(sent_block, BOTH, spread)
        copies = jnp.broadcast_to(moved[None], (side, owned, members))
        segment = lax.all_to_all(
            copies, BOTH, 0, 0, axis_index_groups=plane_groups, tiled=True
        ).reshape(side * owned, members)
        away = half_product(stiff, segment, theirs)
        received = lax.ppermute(away, "col", swap)
        kept = half_product(stiff, segment, mine, received)
        terms = lax.all_to_all(kept, "col", 0, 0, axis_index_groups=same_core, tiled=True)
        return jnp.sum(terms.astype(jnp.float32), axis=0)

    def section(stress_now, state_now):
        slip_rate, deficit = friction(stress_now, state_now, params[1])
        coupled = coupling(deficit.astype(jnp.bfloat16))
        return rates_from(state_now, slip_rate, deficit, coupled, params)

    def total_over(values, axis):
        copies = jnp.broadcast_to(values[None], (side, members))
        return jnp.sum(lax.all_to_all(copies, axis, 0, 0, tiled=True), axis=0)

    full_step = step[None, :]
    first_u, first_p = section(stress, state)
    second_u, second_p = section(stress + full_step * first_u, state + full_step * first_p)
    half_step = 0.5 * full_step
    stress_next = stress + half_step * (first_u + second_u)
    state_next = state + half_step * (first_p + second_p)
    positions = first_patch + jnp.arange(owned, dtype=jnp.int32)
    depth = 0.5 + 1.5 * (positions.astype(jnp.float32) + 0.5) / patch_total
    squared = (depth[:, None] * half_step * (second_u - first_u)) ** 2 + (
        half_step * (second_p - first_p)
    ) ** 2
    partial_sums = jnp.sum(squared, axis=0)
    summed = total_over(total_over(partial_sums, "col"), "row")
    error_norm = jnp.sqrt(summed / (2 * patch_total) + epsilon) / tolerance
    return (stress_next, state_next, error_norm)


def solution(mesh):
    return jax.shard_map(
        body,
        mesh=mesh,
        in_specs=(
            P("row", "col"),
            P(("row", "col")),
            P(("row", "col"), None),
            P(("row", "col"), None),
            P(("row", "col")),
            P(("row", "col")),
            P(("row", "col")),
            P(("row", "col")),
            P(),
        ),
        out_specs=(P(("row", "col"), None), P(("row", "col"), None), P()),
        check_vma=False,
    )
```

time: 513 us -> 180 us (0.35)
  waiting for transfers between devices: 392 us -> 60.1 us
  starting transfers between devices: 0.25 us -> 40.7 us
  blocking collectives: 79.7 us -> 52.7 us
  between operations: 14.2 us -> 0.82 us
  matrix products: 12.7 us -> 0 us
  local copies, waits for them, and re-layouts: 4.53 us -> 13.3 us
  Pallas kernels: 0 us -> 7.91 us
    psum x2 -> x0, waiting for transfers between devices: 192 us -> none  [from_root(): return lax.psum(jnp.where(mine, array, jnp.zeros_like(array)), axis)]
    reduce_scatter x2 -> x0, waiting for transfers between devices: 115 us -> none  [coupling(): lax.psum_scatter(jnp.dot(stiffness, segment, preferred_element_type=jnp.f...]
    all_gather x2 -> x0, waiting for transfers between devices: 85.1 us -> none  [coupling(): gathered_rows = lax.all_gather(sent_block, 'col', axis=0, tiled=True)]
    psum x1 -> x0, blocking collectives: 79.7 us -> none  [body(): summed = lax.psum(partial_sums, ('row', 'col'))]
    all_to_all x0 -> x3, waiting for transfers between devices: none -> 53.9 us  [the longest x2 38.6 us: coupling(): lax.all_to_all(kept, 'col', 0, 0, axis_index_groups=same_core, tiled=True)]
    all_to_all x0 -> x3, blocking collectives: none -> 52.7 us  [the longest x1 32.8 us: coupling(): lax.all_to_all(copies, BOTH, 0, 0, axis_index_groups=plane_groups, tiled=...]
    all_to_all x0 -> x3, starting transfers between devices: none -> 26.9 us  [the longest x1 17.3 us: coupling(): lax.all_to_all(copies, BOTH, 0, 0, axis_index_groups=plane_groups, tiled=...]
    ppermute x0 -> x4, starting transfers between devices: none -> 13.8 us  [the longest x2 8.07 us: coupling(): moved = lax.ppermute(sent_block, BOTH, spread)]
  transfers between devices with their start and end apart: 6 -> 7, of which waited for: 6 -> 7; matrix products, arithmetic and copies ran while one was open for 0% -> 0% of each run, Pallas kernels for 0% -> 0%
where the time goes in v1:
time: 180 us
  waiting for transfers between devices  60.1 us (33%)
  blocking collectives  52.7 us (29%)
  starting transfers between devices  40.7 us (23%)
  local copies, waits for them, and re-layouts  13.3 us (7%)
  Pallas kernels  7.91 us (4%)
  other arithmetic  4.08 us (2%)
    all_to_all x2, waiting for transfers between devices, coupling(): lax.all_to_all(kept, 'col', 0, 0, axis_index_groups=same_core, tiled=True)  38.6 us
    all_to_all x1, blocking collectives, coupling(): lax.all_to_all(copies, BOTH, 0, 0, axis_index_groups=plane_groups, tiled=...  32.8 us
    all_to_all x2, blocking collectives, total_over(): return jnp.sum(lax.all_to_all(copies, axis, 0, 0, tiled=True), axis=0)  19.9 us
    all_to_all x1, starting transfers between devices, coupling(): lax.all_to_all(copies, BOTH, 0, 0, axis_index_groups=plane_groups, tiled=...  17.3 us
    all_to_all x1, waiting for transfers between devices, coupling(): lax.all_to_all(copies, BOTH, 0, 0, axis_index_groups=plane_groups, tiled=...  15.3 us
    unnamed x24, local copies, waits for them, and re-layouts  12.1 us
    all_to_all x2, starting transfers between devices, coupling(): lax.all_to_all(kept, 'col', 0, 0, axis_index_groups=same_core, tiled=True)  9.58 us
    ppermute x2, starting transfers between devices, coupling(): moved = lax.ppermute(sent_block, BOTH, spread)  8.07 us
  transfers between devices with their start and end apart: 7, of which 7 were waited for; matrix products, arithmetic and copies ran while one was open for 0% of the time, Pallas kernels for 0%

profile of v1, /device:TPU:1, one launch (start us, length us, event | category | flops | bytes accessed | tf_op | source)
XLA Modules:
  0.0 179.6 jit_solution(12343026828326315662)
XLA Ops:
  0.6 1.1 subtract_convert_fusion.1
  1.8 4.6 %collective-permute-start = (bf16[144,256]{1,0:T(8,128)(2,1)S(1)}, bf16[144,256]{1,0:T(8,128)(2,1)S(1)}, u32[]{:S(2)}, u32[]{:S(2)}) collective-permute-start(bf16[144,256]{1,0:T(8,128)(2,1)S(1)} %subtract_convert_fusion.1), channel_id=1, source_target_pairs={{0,0},{1,16},{2,32},{3,48},{4,64},{5,80},{6,96},{7,112},{8,128},{9... | collective-permute-start | bytes 221192 | tf_op jit(solution)/shard_map/ppermute | solution.py:77
  6.4 1.4 collective-permute-done
  7.8 1.1 broadcast_in_dim.8
  8.9 17.3 %all-to-all-start = ((bf16[16,144,256]{2,1,0:T(8,128)(2,1)}), bf16[16,144,256]{2,1,0:T(8,128)(2,1)S(1)}, u32[]{:S(2)}, u32[]{:S(2)}) async-start(bf16[16,144,256]{2,1,0:T(8,128)(2,1)} %broadcast_in_dim.8), calls=%async_computation | async-start | bytes 2359296 | tf_op jit(solution)/shard_map/all_to_all | solution.py:79
  26.2 15.3 %all-to-all-done = bf16[16,144,256]{2,1,0:T(8,128)(2,1)S(1)} async-done(((bf16[16,144,256]{2,1,0:T(8,128)(2,1)}), bf16[16,144,256]{2,1,0:T(8,128)(2,1)S(1)}, u32[]{:S(2)}, u32[]{:S(2)}) %all-to-all-start) | async-done | bytes 1179680 | tf_op jit(solution)/shard_map/all_to_all | solution.py:79
  41.5 0.0 copy-start
  41.5 4.0 %copy-done = bf16[2304,2304]{1,0:T(8,128)(2,1)S(1)} copy-done((bf16[2304,2304]{1,0:T(8,128)(2,1)S(1)}, bf16[2304,2304]{1,0:T(8,128)(2,1)}, u32[]{:S(2)}) %copy-start) | copy-done | bytes 10616856
  45.5 0.0 copy-start.1
  45.5 1.6 shard_map.112
  47.0 3.6 %collective-permute-start.1 = (bf16[8,144,256]{2,1,0:T(8,128)(2,1)S(1)}, bf16[8,144,256]{2,1,0:T(8,128)(2,1)S(1)}, u32[]{:S(2)}, u32[]{:S(2)}) collective-permute-start(bf16[8,144,256]{2,1,0:T(8,128)(2,1)S(1)} %shard_map.112), channel_id=1, source_target_pairs={{0,1},{1,0},{2,3},{3,2},{4,5},{5,4},{6,7},{7,6},{8,9},{9,8},{10,11... | collective-permute-start | bytes 1769480 | tf_op jit(solution)/shard_map/ppermute | solution.py:83
  50.7 1.6 collective-permute-done.1.rest_0_
  52.3 0.0 copy-done.1
  52.3 2.4 %shard_map.113 = bf16[8,144,256]{2,1,0:T(8,128)(2,1)} custom-call(s32[1]{0:T(128)} %bitcast.parity_ref, bf16[8,2,144,2304]{3,2,1,0:T(8,128)(2,1)S(1)} %bitcast.5, bf16[2304,256]{1,0:T(8,128)(2,1)S(1)} %bitcast.9, bf16[8,144,256]{2,1,0:T(8,128)(2,1)S(1)} %collective-permute-done.1.rest_0_), custom_call_target="tpu_custom_call" | custom-call | flops 1358954496 | bytes 5308416 | tf_op jit(solution)/shard_map/pallas_call | solution.py:40
  54.7 0.0 copy-start.10
  54.7 0.0 copy-start.11
  54.7 0.0 copy-start.7
  54.7 0.0 copy-start.4
  54.7 0.0 copy-start.5
  54.7 0.0 copy-start.6
  54.7 0.0 copy-start.8
  54.7 0.0 copy-start.9
  54.7 6.0 %all-to-all-start.1 = ((bf16[8,144,256]{2,1,0:T(8,128)(2,1)}), bf16[8,144,256]{2,1,0:T(8,128)(2,1)S(1)}, u32[]{:S(2)}, u32[]{:S(2)}) async-start(bf16[8,144,256]{2,1,0:T(8,128)(2,1)} %shard_map.113), calls=%async_computation.1 | async-start | bytes 1179648 | tf_op jit(solution)/shard_map/all_to_all | solution.py:85
  60.8 0.0 copy-done.10
  60.8 0.0 copy-done.11
  60.8 0.0 copy-done.7
  60.8 19.3 %all-to-all-done.1 = bf16[8,144,256]{2,1,0:T(8,128)(2,1)S(1)} async-done(((bf16[8,144,256]{2,1,0:T(8,128)(2,1)}), bf16[8,144,256]{2,1,0:T(8,128)(2,1)S(1)}, u32[]{:S(2)}, u32[]{:S(2)}) %all-to-all-start.1) | async-done | bytes 589856 | tf_op jit(solution)/shard_map/all_to_all | solution.py:85
  80.2 0.1 convert_reduce_fusion.1
  80.2 0.0 copy-done.4
  80.2 0.0 copy-done.5
  80.3 0.0 copy-done.6
  80.3 0.0 copy-done.8
  80.3 0.0 copy-done.9
  80.3 1.1 multiply_add_fusion
  81.3 0.1 subtract_convert_fusion
  81.4 3.5 %collective-permute-start.2 = (bf16[144,256]{1,0:T(8,128)(2,1)S(1)}, bf16[144,256]{1,0:T(8,128)(2,1)S(1)}, u32[]{:S(2)}, u32[]{:S(2)}) collective-permute-start(bf16[144,256]{1,0:T(8,128)(2,1)S(1)} %subtract_convert_fusion), channel_id=1, source_target_pairs={{0,0},{1,16},{2,32},{3,48},{4,64},{5,80},{6,96},{7,112},{8,128},{9... | collective-permute-start | bytes 221192 | tf_op jit(solution)/shard_map/ppermute | solution.py:77
  84.9 1.6 collective-permute-done.2
  86.5 0.1 broadcast_in_dim.9
  86.6 32.8 %all_to_all.32 = bf16[16,144,256]{2,1,0:T(8,128)(2,1)S(1)} all-to-all(bf16[16,144,256]{2,1,0:T(8,128)(2,1)S(1)} %broadcast_in_dim.9), channel_id=1, replica_groups={{0,16,32,48,64,80,96,112,128,144,160,176,192,208,224,240},{17,1,49,33,8..., dimensions={0} | all-to-all | bytes 2359296 | tf_op jit(solution)/shard_map/all_to_all | solution.py:79
  119.4 0.0 copy-start.2
  119.4 4.0 %copy-done.2 = bf16[2304,2304]{1,0:T(8,128)(2,1)S(1)} copy-done((bf16[2304,2304]{1,0:T(8,128)(2,1)S(1)}, bf16[2304,2304]{1,0:T(8,128)(2,1)}, u32[]{:S(2)}) %copy-start.2) | copy-done | bytes 10616856
  123.4 1.6 shard_map.114
  124.9 2.1 %collective-permute-start.3 = (bf16[8,144,256]{2,1,0:T(8,128)(2,1)S(1)}, bf16[8,144,256]{2,1,0:T(8,128)(2,1)S(1)}, u32[]{:S(2)}, u32[]{:S(2)}) collective-permute-start(bf16[8,144,256]{2,1,0:T(8,128)(2,1)S(1)} %shard_map.114), channel_id=1, source_target_pairs={{0,1},{1,0},{2,3},{3,2},{4,5},{5,4},{6,7},{7,6},{8,9},{9,8},{10,11... | collective-permute-start | bytes 1769480 | tf_op jit(solution)/shard_map/ppermute | solution.py:83
  127.1 1.6 collective-permute-done.3.rest_0_
  128.7 0.0 copy-start.3
  128.7 4.0 %copy-done.3 = bf16[2304,2304]{1,0:T(8,128)(2,1)S(1)} copy-done((bf16[2304,2304]{1,0:T(8,128)(2,1)S(1)}, bf16[2304,2304]{1,0:T(8,128)(2,1)}, u32[]{:S(2)}) %copy-start.3) | copy-done | bytes 10616856
  132.7 2.4 %shard_map.115 = bf16[8,144,256]{2,1,0:T(8,128)(2,1)} custom-call(s32[1]{0:T(128)} %bitcast.parity_ref, bf16[8,2,144,2304]{3,2,1,0:T(8,128)(2,1)S(1)} %bitcast.7, bf16[2304,256]{1,0:T(8,128)(2,1)S(1)} %bitcast.11, bf16[8,144,256]{2,1,0:T(8,128)(2,1)S(1)} %collective-permute-done.3.rest_0_), custom_call_target="tpu_custom_call" | custom-call | flops 1358954496 | bytes 5308416 | tf_op jit(solution)/shard_map/pallas_call | solution.py:40
  135.1 3.5 %all-to-all-start.3 = ((bf16[8,144,256]{2,1,0:T(8,128)(2,1)}), bf16[8,144,256]{2,1,0:T(8,128)(2,1)S(1)}, u32[]{:S(2)}, u32[]{:S(2)}) async-start(bf16[8,144,256]{2,1,0:T(8,128)(2,1)} %shard_map.115), calls=%async_computation.3 | async-start | bytes 1179648 | tf_op jit(solution)/shard_map/all_to_all | solution.py:85
  138.7 19.3 %all-to-all-done.3 = bf16[8,144,256]{2,1,0:T(8,128)(2,1)S(1)} async-done(((bf16[8,144,256]{2,1,0:T(8,128)(2,1)}), bf16[8,144,256]{2,1,0:T(8,128)(2,1)S(1)}, u32[]{:S(2)}, u32[]{:S(2)}) %all-to-all-start.3) | async-done | bytes 589856 | tf_op jit(solution)/shard_map/all_to_all | solution.py:85
  158.0 0.1 convert_reduce_fusion
  158.1 1.0 add_reduce_fusion
  159.1 10.3 %all_to_all.33 = f32[16,1,256]{2,1,0:T(1,128)S(1)} all-to-all(f32[16,1,256]{2,1,0:T(1,128)S(1)} %broadcast_in_dim.10), channel_id=1, replica_groups=mesh['row'=16,'col'=16] {'col'}, dimensions={0} | all-to-all | bytes 32768 | tf_op jit(solution)/shard_map/all_to_all | solution.py:95
  169.4 9.6 %all_to_all.34 = f32[16,1,256]{2,1,0:T(1,128)S(1)} all-to-all(f32[16,1,256]{2,1,0:T(1,128)S(1)} %broadcast_in_dim.11), channel_id=1, replica_groups=mesh['row'=16,'col'=16] {'row'}, dimensions={0} | all-to-all | bytes 32768 | tf_op jit(solution)/shard_map/all_to_all | solution.py:95
  179.1 0.6 sqrt_multiply_fusion
  (8 shorter events, 0.1 us)
Async XLA Ops:
  1.8 6.0 %collective-permute-start = (bf16[144,256]{1,0:T(8,128)(2,1)S(1)}, bf16[144,256]{1,0:T(8,128)(2,1)S(1)}, u32[]{:S(2)}, u32[]{:S(2)}) collective-permute-start(bf16[144,256]{1,0:T(8,128)(2,1)S(1)} %subtract_convert_fusion.1), channel_id=1, source_target_pairs={{0,0},{1,16},{2,32},{3,48},{4,64},{5,80},{6,96},{7,112},{8,128},{9... | collective-permute-start | bytes 221192 | tf_op jit(solution)/shard_map/ppermute | solution.py:77
  8.9 32.6 %all-to-all-start = ((bf16[16,144,256]{2,1,0:T(8,128)(2,1)}), bf16[16,144,256]{2,1,0:T(8,128)(2,1)S(1)}, u32[]{:S(2)}, u32[]{:S(2)}) async-start(bf16[16,144,256]{2,1,0:T(8,128)(2,1)} %broadcast_in_dim.8), calls=%async_computation | async-start | bytes 2359296 | tf_op jit(solution)/shard_map/all_to_all | solution.py:79
  41.5 4.0 %copy-start = (bf16[2304,2304]{1,0:T(8,128)(2,1)S(1)}, bf16[2304,2304]{1,0:T(8,128)(2,1)}, u32[]{:S(2)}) copy-start(bf16[2304,2304]{1,0:T(8,128)(2,1)} %param.9) | copy-start | bytes 31850500
  45.5 6.8 %copy-start.1 = (bf16[2304,2304]{1,0:T(8,128)(2,1)S(1)}, bf16[2304,2304]{1,0:T(8,128)(2,1)}, u32[]{:S(2)}) copy-start(bf16[2304,2304]{1,0:T(8,128)(2,1)} %param.9) | copy-start | bytes 31850500
  47.0 5.2 %collective-permute-start.1 = (bf16[8,144,256]{2,1,0:T(8,128)(2,1)S(1)}, bf16[8,144,256]{2,1,0:T(8,128)(2,1)S(1)}, u32[]{:S(2)}, u32[]{:S(2)}) collective-permute-start(bf16[8,144,256]{2,1,0:T(8,128)(2,1)S(1)} %shard_map.112), channel_id=1, source_target_pairs={{0,1},{1,0},{2,3},{3,2},{4,5},{5,4},{6,7},{7,6},{8,9},{9,8},{10,11... | collective-permute-start | bytes 1769480 | tf_op jit(solution)/shard_map/ppermute | solution.py:83
  54.7 6.1 %copy-start.10 = (f32[144]{0:T(256)S(1)}, f32[144]{0:T(256)}, u32[]{:S(2)}) copy-start(f32[144]{0:T(256)} %param.10) | copy-start | bytes 1732
  54.7 6.1 %copy-start.11 = (f32[144]{0:T(256)S(1)}, f32[144]{0:T(256)}, u32[]{:S(2)}) copy-start(f32[144]{0:T(256)} %param.16) | copy-start | bytes 1732
  54.7 6.1 %copy-start.7 = (f32[256]{0:T(256)S(1)}, f32[256]{0:T(256)}, u32[]{:S(2)}) copy-start(f32[256]{0:T(256)} %param.17) | copy-start | bytes 3076
  54.7 25.5 %copy-start.4 = (f32[144,256]{1,0:T(8,128)S(1)}, f32[144,256]{1,0:T(8,128)}, u32[]{:S(2)}) copy-start(f32[144,256]{1,0:T(8,128)} %param.12) | copy-start | bytes 442372
  54.7 25.5 %copy-start.5 = (f32[144,256]{1,0:T(8,128)S(1)}, f32[144,256]{1,0:T(8,128)}, u32[]{:S(2)}) copy-start(f32[144,256]{1,0:T(8,128)} %param.11) | copy-start | bytes 442372
  54.7 25.5 %copy-start.6 = (f32[144]{0:T(256)S(1)}, f32[144]{0:T(256)}, u32[]{:S(2)}) copy-start(f32[144]{0:T(256)} %param.13) | copy-start | bytes 1732
  54.7 25.5 %copy-start.8 = (f32[144]{0:T(256)S(1)}, f32[144]{0:T(256)}, u32[]{:S(2)}) copy-start(f32[144]{0:T(256)} %param.15) | copy-start | bytes 1732
  54.7 25.5 %copy-start.9 = (f32[144]{0:T(256)S(1)}, f32[144]{0:T(256)}, u32[]{:S(2)}) copy-start(f32[144]{0:T(256)} %param.14) | copy-start | bytes 1732
  54.7 25.4 %all-to-all-start.1 = ((bf16[8,144,256]{2,1,0:T(8,128)(2,1)}), bf16[8,144,256]{2,1,0:T(8,128)(2,1)S(1)}, u32[]{:S(2)}, u32[]{:S(2)}) async-start(bf16[8,144,256]{2,1,0:T(8,128)(2,1)} %shard_map.113), calls=%async_computation.1 | async-start | bytes 1179648 | tf_op jit(solution)/shard_map/all_to_all | solution.py:85
  81.4 5.1 %collective-permute-start.2 = (bf16[144,256]{1,0:T(8,128)(2,1)S(1)}, bf16[144,256]{1,0:T(8,128)(2,1)S(1)}, u32[]{:S(2)}, u32[]{:S(2)}) collective-permute-start(bf16[144,256]{1,0:T(8,128)(2,1)S(1)} %subtract_convert_fusion), channel_id=1, source_target_pairs={{0,0},{1,16},{2,32},{3,48},{4,64},{5,80},{6,96},{7,112},{8,128},{9... | collective-permute-start | bytes 221192 | tf_op jit(solution)/shard_map/ppermute | solution.py:77
  119.4 4.0 %copy-start.2 = (bf16[2304,2304]{1,0:T(8,128)(2,1)S(1)}, bf16[2304,2304]{1,0:T(8,128)(2,1)}, u32[]{:S(2)}) copy-start(bf16[2304,2304]{1,0:T(8,128)(2,1)} %param.9) | copy-start | bytes 31850500
  124.9 3.8 %collective-permute-start.3 = (bf16[8,144,256]{2,1,0:T(8,128)(2,1)S(1)}, bf16[8,144,256]{2,1,0:T(8,128)(2,1)S(1)}, u32[]{:S(2)}, u32[]{:S(2)}) collective-permute-start(bf16[8,144,256]{2,1,0:T(8,128)(2,1)S(1)} %shard_map.114), channel_id=1, source_target_pairs={{0,1},{1,0},{2,3},{3,2},{4,5},{5,4},{6,7},{7,6},{8,9},{9,8},{10,11... | collective-permute-start | bytes 1769480 | tf_op jit(solution)/shard_map/ppermute | solution.py:83
  128.7 4.0 %copy-start.3 = (bf16[2304,2304]{1,0:T(8,128)(2,1)S(1)}, bf16[2304,2304]{1,0:T(8,128)(2,1)}, u32[]{:S(2)}) copy-start(bf16[2304,2304]{1,0:T(8,128)(2,1)} %param.9) | copy-start | bytes 31850500
  135.1 22.9 %all-to-all-start.3 = ((bf16[8,144,256]{2,1,0:T(8,128)(2,1)}), bf16[8,144,256]{2,1,0:T(8,128)(2,1)S(1)}, u32[]{:S(2)}, u32[]{:S(2)}) async-start(bf16[8,144,256]{2,1,0:T(8,128)(2,1)} %shard_map.115), calls=%async_computation.3 | async-start | bytes 1179648 | tf_op jit(solution)/shard_map/all_to_all | solution.py:85

commit v2 on v1

v2 whole, which is shorter than its diff:
```python
import jax
import jax.numpy as jnp
from jax import lax
from jax.experimental import pallas as pl
from jax.experimental.pallas import tpu as pltpu
from jax.sharding import PartitionSpec as P

tolerance = 0.01
epsilon = 1e-06
VMEM_LIMIT = 16 << 20
BOTH = ("row", "col")


def friction(stress_now, state_now, plate_vel):
    slip_rate = 2.0 * jnp.sinh(stress_now) * jnp.exp(-state_now)
    return (slip_rate, slip_rate - plate_vel[:, None])


def rates_from(state_now, slip_rate, deficit, coupled, params):
    diag_stiff, plate_vel, gain_now, heal_now, ratio_now = params
    stress_rate = gain_now[:, None] * (-diag_stiff[:, None] * deficit - coupled)
    state_rate = heal_now[:, None] * (jnp.exp(-ratio_now[:, None] * state_now) - slip_rate)
    return (stress_rate, state_rate)


def ring_distance(first, second, size):
    return min((first - second) % size, (second - first) % size)


def landing_rows(side, width):
    layers = side // 2
    table = []
    for a in range(side):
        far = sorted(
            range(side), key=lambda b: (-ring_distance(b // 2, a // 2, layers), a ^ b)
        )
        near = sorted(
            range(side),
            key=lambda r: (
                ring_distance(r // width, a // width, width)
                + ring_distance(r % width, a % width, width),
                a ^ r,
            ),
        )
        rows = dict(zip(far, near))
        table.append([rows[b] for b in range(side)])
    return table


def resident(stiff):
    def kernel(stiff_ref, out_ref, done):
        copy = pltpu.make_async_copy(stiff_ref, out_ref, done)
        copy.start()
        copy.wait()

    return pl.pallas_call(
        kernel,
        out_shape=jax.ShapeDtypeStruct(stiff.shape, stiff.dtype),
        in_specs=[pl.BlockSpec(memory_space=pltpu.HBM)],
        out_specs=pl.BlockSpec(memory_space=pltpu.VMEM),
        scratch_shapes=[pltpu.SemaphoreType.DMA],
        compiler_params=pltpu.CompilerParams(vmem_limit_bytes=16 << 20),
        cost_estimate=pl.CostEstimate(
            flops=0, bytes_accessed=4 * stiff.size, transcendentals=0
        ),
    )(stiff)


def half_product(stiff, segment, swapped, dtype):
    half, _, owned, depth = stiff.shape
    members = segment.shape[1]

    def kernel(stiff_ref, segment_ref, out_ref, kept_ref):
        core = (lax.axis_index("col") + swapped) % 2
        rows = stiff_ref[:, core].reshape(half * owned, depth)
        product = jnp.dot(rows, segment_ref[...], preferred_element_type=jnp.float32)
        out_ref[...] = product.reshape(half, owned, members).astype(dtype)

    vmem = pl.BlockSpec(memory_space=pltpu.VMEM)
    return pl.pallas_call(
        kernel,
        out_shape=(
            jax.ShapeDtypeStruct((half, owned, members), dtype),
            jax.ShapeDtypeStruct(stiff.shape, stiff.dtype),
        ),
        in_specs=[vmem, vmem],
        out_specs=(vmem, vmem),
        input_output_aliases={0: 1},
        compiler_params=pltpu.CompilerParams(vmem_limit_bytes=VMEM_LIMIT),
        cost_estimate=pl.CostEstimate(
            flops=2 * half * owned * depth * members,
            bytes_accessed=2 * half * owned * depth,
            transcendentals=0,
        ),
    )(stiff, segment)


def body(
    stiffness, self_stiffness, stress, state, plate_rate, stress_gain, heal_rate, ab_ratio, step
):
    owned, members = stress.shape
    side = lax.axis_size("row")
    layers = side // 2
    row_index = lax.axis_index("row")
    col_index = lax.axis_index("col")
    patch_total = owned * side * side
    params = (self_stiffness, plate_rate, stress_gain, heal_rate, ab_ratio)
    first_patch = (row_index * side + col_index) * owned

    everyone = range(side)
    rows = landing_rows(side, 4)
    spread = [(a * side + b, rows[a][b] * side + a) for a in everyone for b in everyone]
    plane_groups = [[rows[a][b] * side + a for b in everyone] for a in everyone]
    same_core = [[2 * z + core for z in range(layers)] for core in range(2)]
    swap = [(c, c ^ 1) for c in everyone]
    stiff = stiffness.reshape(layers, 2, owned, side * owned)
    positions = first_patch + jnp.arange(owned, dtype=jnp.int32)
    depth = 0.5 + 1.5 * (positions.astype(jnp.float32) + 0.5) / patch_total

    def coupling(sent_block, stiff, late):
        moved = lax.ppermute(sent_block, BOTH, spread)
        copies = jnp.broadcast_to(moved[None], (side, owned, members))
        copies, stiff, late = lax.optimization_barrier((copies, stiff, late))
        segment = lax.all_to_all(
            copies, BOTH, 0, 0, axis_index_groups=plane_groups, tiled=True
        ).reshape(side * owned, members)
        segment, stiff, late = lax.optimization_barrier((segment, stiff, late))
        away, stiff = half_product(stiff, segment, 1, jnp.bfloat16)
        received = lax.ppermute(away, "col", swap)
        own, stiff = half_product(stiff, segment, 0, jnp.float32)
        kept = (own + received.astype(jnp.float32)).astype(jnp.bfloat16)
        kept, stiff, late = lax.optimization_barrier((kept, stiff, late))
        terms = lax.all_to_all(kept, "col", 0, 0, axis_index_groups=same_core, tiled=True)
        terms, stiff, late = lax.optimization_barrier((terms, stiff, late))
        return jnp.sum(terms.astype(jnp.float32), axis=0), stiff, late

    def section(stress_now, state_now, stiff, late):
        params = late[:5]
        slip_rate, deficit = friction(stress_now, state_now, plate_rate)
        late = (*late, stress_now, state_now)
        coupled, stiff, late = coupling(deficit.astype(jnp.bfloat16), stiff, late)
        *late, stress_now, state_now = late
        slip_rate, deficit = friction(stress_now, state_now, late[1])
        tendencies = rates_from(state_now, slip_rate, deficit, coupled, tuple(late[:5]))
        return tendencies, stiff, tuple(late)

    def total_over(values, axis):
        copies = jnp.broadcast_to(values[None], (side, members))
        return jnp.sum(lax.all_to_all(copies, axis, 0, 0, tiled=True), axis=0)

    depth, stiff = lax.optimization_barrier((depth, stiff))
    late = (*params, step, depth, stress, state)
    (first_u, first_p), stiff, late = section(stress, state, resident(stiff), late)
    *_, step, depth, stress, state = late
    full_step = step[None, :]
    late = (*late, first_u, first_p)
    (second_u, second_p), stiff, late = section(
        stress + full_step * first_u, state + full_step * first_p, stiff, late
    )
    *_, step, depth, stress, state, first_u, first_p = late
    half_step = 0.5 * step[None, :]
    stress_next = stress + half_step * (first_u + second_u)
    state_next = state + half_step * (first_p + second_p)
    squared = (depth[:, None] * half_step * (second_u - first_u)) ** 2 + (
        half_step * (second_p - first_p)
    ) ** 2
    partial_sums = jnp.sum(squared, axis=0)
    summed = total_over(total_over(partial_sums, "col"), "row")
    error_norm = jnp.sqrt(summed / (2 * patch_total) + epsilon) / tolerance
    return (stress_next, state_next, error_norm)


def solution(mesh):
    return jax.shard_map(
        body,
        mesh=mesh,
        in_specs=(
            P("row", "col"),
            P(("row", "col")),
            P(("row", "col"), None),
            P(("row", "col"), None),
            P(("row", "col")),
            P(("row", "col")),
            P(("row", "col")),
            P(("row", "col")),
            P(),
        ),
        out_specs=(P(("row", "col"), None), P(("row", "col"), None), P()),
        check_vma=False,
    )
```

time: 180 us -> 153 us (0.85)
  blocking collectives: 52.7 us -> 118 us
  waiting for transfers between devices: 60.1 us -> 4.94 us
  starting transfers between devices: 40.7 us -> 14 us
  local copies, waits for them, and re-layouts: 13.3 us -> 4.25 us
    all_to_all x3 -> x0, waiting for transfers between devices: 53.9 us -> none  [the longest x2 38.6 us: coupling(): lax.all_to_all(kept, 'col', 0, 0, axis_index_groups=same_core, tiled=True)]
    all_to_all x0 -> x2, blocking collectives: none -> 48.6 us  [coupling(): lax.all_to_all(kept, 'col', 0, 0, axis_index_groups=same_core, tiled=True)]
    all_to_all x3 -> x0, starting transfers between devices: 26.9 us -> none  [the longest x1 17.3 us: coupling(): lax.all_to_all(copies, BOTH, 0, 0, axis_index_groups=plane_groups, tiled=...]
    all_to_all x1 -> x2, blocking collectives: 32.8 us -> 47.6 us  [coupling(): lax.all_to_all(copies, BOTH, 0, 0, axis_index_groups=plane_groups, tiled=...]
    unnamed x24 -> x18, local copies, waits for them, and re-layouts: 12.1 us -> 4.07 us
    ppermute x2, waiting for transfers between devices: 3.26 us -> 0.12 us  [coupling(): received = lax.ppermute(away, 'col', swap)]
    ppermute x2, starting transfers between devices: 8.07 us -> 10.9 us  [coupling(): moved = lax.ppermute(sent_block, BOTH, spread)]
    ppermute x2, starting transfers between devices: 5.75 us -> 3.05 us  [coupling(): received = lax.ppermute(away, 'col', swap)]
  transfers between devices with their start and end apart: 7 -> 4, of which waited for: 7 -> 3; matrix products, arithmetic and copies ran while one was open for 0% -> 0% of each run, Pallas kernels for 0% -> 3%
where the time goes in v2:
time: 153 us
  blocking collectives  118 us (77%)
  starting transfers between devices  14 us (9%)
  Pallas kernels  7.1 us (5%)
  waiting for transfers between devices  4.94 us (3%)
  local copies, waits for them, and re-layouts  4.25 us (3%)
  other arithmetic  3.59 us (2%)
    all_to_all x2, blocking collectives, coupling(): lax.all_to_all(kept, 'col', 0, 0, axis_index_groups=same_core, tiled=True)  48.6 us
    all_to_all x2, blocking collectives, coupling(): lax.all_to_all(copies, BOTH, 0, 0, axis_index_groups=plane_groups, tiled=...  47.6 us
    all_to_all x2, blocking collectives, total_over(): return jnp.sum(lax.all_to_all(copies, axis, 0, 0, tiled=True), axis=0)  22.2 us
    ppermute x2, starting transfers between devices, coupling(): moved = lax.ppermute(sent_block, BOTH, spread)  10.9 us
    pallas_call x4, Pallas kernels, half_product(): pl.pallas_call(kernel, out_shape=(jax.ShapeDtypeStruct((half, owned, memb...  6.21 us
    ppermute x2, waiting for transfers between devices, coupling(): moved = lax.ppermute(sent_block, BOTH, spread)  4.82 us
    unnamed x18, local copies, waits for them, and re-layouts  4.07 us
  transfers between devices with their start and end apart: 4, of which 3 were waited for; matrix products, arithmetic and copies ran while one was open for 0% of the time, Pallas kernels for 3%

profile of v2, /device:TPU:1, one launch (start us, length us, event | category | flops | bytes accessed | tf_op | source)
XLA Modules:
  0.0 153.1 jit_solution(12045898571594310987)
XLA Ops:
  0.6 1.1 fusion.19
  1.8 6.9 %collective-permute-start = (bf16[144,256]{1,0:T(8,128)(2,1)S(1)}, bf16[144,256]{1,0:T(8,128)(2,1)S(1)}, u32[]{:S(2)}, u32[]{:S(2)}) collective-permute-start(bf16[144,256]{1,0:T(8,128)(2,1)S(1)} %fusion.19), channel_id=1, source_target_pairs={{0,224},{1,160},{2,240},{3,96},{4,80},{5,112},{6,48},{7,64},{8,0},... | collective-permute-start | bytes 221192 | tf_op jit(solution)/shard_map/ppermute | solution.py:121
  8.6 0.0 copy-start
  8.6 4.0 %copy-done = bf16[2304,2304]{1,0:T(8,128)(2,1)S(1)} copy-done((bf16[2304,2304]{1,0:T(8,128)(2,1)S(1)}, bf16[2304,2304]{1,0:T(8,128)(2,1)}, u32[]{:S(2)}) %copy-start) | copy-done | bytes 10616856
  12.6 0.9 shard_map.112.stiff_ref
  13.5 0.0 collective-permute-done
  13.5 0.1 broadcast_in_dim.8
  13.6 24.3 %all_to_all.32 = bf16[16,144,256]{2,1,0:T(8,128)(2,1)S(1)} all-to-all(bf16[16,144,256]{2,1,0:T(8,128)(2,1)S(1)} %broadcast_in_dim.8), channel_id=1, replica_groups={{224,160,240,96,80,112,48,64,0,16,192,32,128,208,144,176},{177,241,113,..., dimensions={0} | all-to-all | bytes 2359296 | tf_op jit(solution)/shard_map/all_to_all | solution.py:124
  38.0 1.5 %shard_map.113 = (bf16[8,144,256]{2,1,0:T(8,128)(2,1)S(1)}, bf16[8,2,144,2304]{3,2,1,0:T(8,128)(2,1)S(1)}) custom-call(bf16[8,2,144,2304]{3,2,1,0:T(8,128)(2,1)S(1)} %shard_map.112.stiff_ref, bf16[2304,256]{1,0:T(8,128)(2,1)S(1)} %bitcast.3), custom_call_target="tpu_custom_call", output_to_operand_aliasing={{1}: (0, {})} | custom-call | flops 1358954496 | bytes 5308416 | tf_op jit(solution)/shard_map/pallas_call | solution.py:80
  39.5 0.8 collective-permute-start.1
  40.3 1.6 %shard_map.114 = (f32[8,144,256]{2,1,0:T(8,128)S(1)}, bf16[8,2,144,2304]{3,2,1,0:T(8,128)(2,1)S(1)}) custom-call(bf16[8,2,144,2304]{3,2,1,0:T(8,128)(2,1)S(1)} %get-tuple-element.139.stiff_ref, bf16[2304,256]{1,0:T(8,128)(2,1)S(1)} %bitcast.4), custom_call_target="tpu_custom_call", output_to_operand_aliasing={{1}: (0, {})} | custom-call | flops 1358954496 | bytes 5308416 | tf_op jit(solution)/shard_map/pallas_call | solution.py:80
  41.9 0.1 collective-permute-done.1
  42.0 0.1 add_convert_fusion.1
  42.1 0.0 copy-start.5
  42.1 0.0 copy-start.6
  42.1 0.0 copy-start.1
  42.2 0.0 copy-start.2
  42.2 0.0 copy-start.3
  42.2 0.0 copy-start.4
  42.2 0.0 copy-start.7
  42.2 0.0 copy-start.8
  42.2 27.0 %all_to_all.33 = bf16[8,144,256]{2,1,0:T(8,128)(2,1)S(1)} all-to-all(bf16[8,144,256]{2,1,0:T(8,128)(2,1)S(1)} %add_convert_fusion.1), channel_id=1, replica_groups={{0,2,4,6,8,10,12,14},{1,3,5,7,9,11,13,15},{16,18,20,22,24,26,28,30},{17..., dimensions={0} | all-to-all | bytes 1179648 | tf_op jit(solution)/shard_map/all_to_all | solution.py:133
  69.2 0.0 copy-done.5
  69.2 0.0 copy-done.6
  69.2 0.1 convert_reduce_fusion.1
  69.3 0.0 copy-done.1
  69.3 0.0 copy-done.2
  69.3 0.0 copy-done.3
  69.3 0.0 copy-done.4
  69.3 0.0 copy-done.7
  69.3 0.0 copy-done.8
  69.3 0.4 fusion.18
  69.7 4.1 %collective-permute-start.2 = (bf16[144,256]{1,0:T(8,128)(2,1)S(1)}, bf16[144,256]{1,0:T(8,128)(2,1)S(1)}, u32[]{:S(2)}, u32[]{:S(2)}) collective-permute-start(bf16[144,256]{1,0:T(8,128)(2,1)S(1)} %get-tuple-element.241), channel_id=1, source_target_pairs={{0,224},{1,160},{2,240},{3,96},{4,80},{5,112},{6,48},{7,64},{8,0},... | collective-permute-start | bytes 221192 | tf_op jit(solution)/shard_map/ppermute | solution.py:121
  73.8 4.8 %collective-permute-done.2 = bf16[144,256]{1,0:T(8,128)(2,1)S(1)} collective-permute-done((bf16[144,256]{1,0:T(8,128)(2,1)S(1)}, bf16[144,256]{1,0:T(8,128)(2,1)S(1)}, u32[]{:S(2)}, u32[]{:S(2)}) %collective-permute-start.2) | collective-permute-done | bytes 73760 | tf_op jit(solution)/shard_map/ppermute | solution.py:121
  78.6 0.1 broadcast_in_dim.9
  78.7 23.3 %all_to_all.34 = bf16[16,144,256]{2,1,0:T(8,128)(2,1)S(1)} all-to-all(bf16[16,144,256]{2,1,0:T(8,128)(2,1)S(1)} %broadcast_in_dim.9), channel_id=1, replica_groups={{224,160,240,96,80,112,48,64,0,16,192,32,128,208,144,176},{177,241,113,..., dimensions={0} | all-to-all | bytes 2359296 | tf_op jit(solution)/shard_map/all_to_all | solution.py:124
  102.0 1.5 %shard_map.115 = (bf16[8,144,256]{2,1,0:T(8,128)(2,1)S(1)}, bf16[8,2,144,2304]{3,2,1,0:T(8,128)(2,1)S(1)}) custom-call(bf16[8,2,144,2304]{3,2,1,0:T(8,128)(2,1)S(1)} %get-tuple-element.195.stiff_ref, bf16[2304,256]{1,0:T(8,128)(2,1)S(1)} %bitcast.5), custom_call_target="tpu_custom_call", output_to_operand_aliasing={{1}: (0, {})} | custom-call | flops 1358954496 | bytes 5308416 | tf_op jit(solution)/shard_map/pallas_call | solution.py:80
  103.5 2.2 %collective-permute-start.3 = (bf16[8,144,256]{2,1,0:T(8,128)(2,1)S(1)}, bf16[8,144,256]{2,1,0:T(8,128)(2,1)S(1)}, u32[]{:S(2)}, u32[]{:S(2)}) collective-permute-start(bf16[8,144,256]{2,1,0:T(8,128)(2,1)S(1)} %get-tuple-element.199), channel_id=1, source_target_pairs={{0,1},{1,0},{2,3},{3,2},{4,5},{5,4},{6,7},{7,6},{8,9},{9,8},{10,11... | collective-permute-start | bytes 1769480 | tf_op jit(solution)/shard_map/ppermute | solution.py:129
  105.7 1.6 %shard_map.116 = (f32[8,144,256]{2,1,0:T(8,128)S(1)}, bf16[8,2,144,2304]{3,2,1,0:T(8,128)(2,1)S(1)}) custom-call(bf16[8,2,144,2304]{3,2,1,0:T(8,128)(2,1)S(1)} %get-tuple-element.197.stiff_ref, bf16[2304,256]{1,0:T(8,128)(2,1)S(1)} %bitcast.6), custom_call_target="tpu_custom_call", output_to_operand_aliasing={{1}: (0, {})} | custom-call | flops 1358954496 | bytes 5308416 | tf_op jit(solution)/shard_map/pallas_call | solution.py:80
  107.3 0.1 collective-permute-done.3
  107.4 0.1 add_convert_fusion
  107.5 21.6 %all_to_all.35 = bf16[8,144,256]{2,1,0:T(8,128)(2,1)S(1)} all-to-all(bf16[8,144,256]{2,1,0:T(8,128)(2,1)S(1)} %add_convert_fusion), channel_id=1, replica_groups={{0,2,4,6,8,10,12,14},{1,3,5,7,9,11,13,15},{16,18,20,22,24,26,28,30},{17..., dimensions={0} | all-to-all | bytes 1179648 | tf_op jit(solution)/shard_map/all_to_all | solution.py:133
  129.2 0.1 convert_reduce_fusion
  129.2 1.0 add_reduce_fusion
  130.2 11.3 %all_to_all.36 = f32[16,1,256]{2,1,0:T(1,128)S(1)} all-to-all(f32[16,1,256]{2,1,0:T(1,128)S(1)} %broadcast_in_dim.10), channel_id=1, replica_groups=mesh['row'=16,'col'=16] {'col'}, dimensions={0} | all-to-all | bytes 32768 | tf_op jit(solution)/shard_map/all_to_all | solution.py:149
  141.5 10.9 %all_to_all.37 = f32[16,1,256]{2,1,0:T(1,128)S(1)} all-to-all(f32[16,1,256]{2,1,0:T(1,128)S(1)} %broadcast_in_dim.11), channel_id=1, replica_groups=mesh['row'=16,'col'=16] {'row'}, dimensions={0} | all-to-all | bytes 32768 | tf_op jit(solution)/shard_map/all_to_all | solution.py:149
  152.5 0.6 sqrt_multiply_fusion
  (10 shorter events, 0.1 us)
Async XLA Ops:
  1.8 11.8 %collective-permute-start = (bf16[144,256]{1,0:T(8,128)(2,1)S(1)}, bf16[144,256]{1,0:T(8,128)(2,1)S(1)}, u32[]{:S(2)}, u32[]{:S(2)}) collective-permute-start(bf16[144,256]{1,0:T(8,128)(2,1)S(1)} %fusion.19), channel_id=1, source_target_pairs={{0,224},{1,160},{2,240},{3,96},{4,80},{5,112},{6,48},{7,64},{8,0},... | collective-permute-start | bytes 221192 | tf_op jit(solution)/shard_map/ppermute | solution.py:121
  8.6 4.0 %copy-start = (bf16[2304,2304]{1,0:T(8,128)(2,1)S(1)}, bf16[2304,2304]{1,0:T(8,128)(2,1)}, u32[]{:S(2)}) copy-start(bf16[2304,2304]{1,0:T(8,128)(2,1)} %param.9) | copy-start | bytes 31850500
  39.5 2.5 %collective-permute-start.1 = (bf16[8,144,256]{2,1,0:T(8,128)(2,1)S(1)}, bf16[8,144,256]{2,1,0:T(8,128)(2,1)S(1)}, u32[]{:S(2)}, u32[]{:S(2)}) collective-permute-start(bf16[8,144,256]{2,1,0:T(8,128)(2,1)S(1)} %get-tuple-element.141), channel_id=1, source_target_pairs={{0,1},{1,0},{2,3},{3,2},{4,5},{5,4},{6,7},{7,6},{8,9},{9,8},{10,11... | collective-permute-start | bytes 1769480 | tf_op jit(solution)/shard_map/ppermute | solution.py:129
  42.1 27.1 %copy-start.5 = (f32[144]{0:T(256)S(1)}, f32[144]{0:T(256)}, u32[]{:S(2)}) copy-start(f32[144]{0:T(256)} %param.10) | copy-start | bytes 1732
  42.1 27.0 %copy-start.6 = (f32[144]{0:T(256)S(1)}, f32[144]{0:T(256)}, u32[]{:S(2)}) copy-start(f32[144]{0:T(256)} %param.16) | copy-start | bytes 1732
  42.1 27.1 %copy-start.1 = (f32[144,256]{1,0:T(8,128)S(1)}, f32[144,256]{1,0:T(8,128)}, u32[]{:S(2)}) copy-start(f32[144,256]{1,0:T(8,128)} %param.11) | copy-start | bytes 442372
  42.2 27.1 %copy-start.2 = (f32[144,256]{1,0:T(8,128)S(1)}, f32[144,256]{1,0:T(8,128)}, u32[]{:S(2)}) copy-start(f32[144,256]{1,0:T(8,128)} %param.12) | copy-start | bytes 442372
  42.2 27.1 %copy-start.3 = (f32[144]{0:T(256)S(1)}, f32[144]{0:T(256)}, u32[]{:S(2)}) copy-start(f32[144]{0:T(256)} %param.13) | copy-start | bytes 1732
  42.2 27.1 %copy-start.4 = (f32[256]{0:T(256)S(1)}, f32[256]{0:T(256)}, u32[]{:S(2)}) copy-start(f32[256]{0:T(256)} %param.17) | copy-start | bytes 3076
  42.2 27.1 %copy-start.7 = (f32[144]{0:T(256)S(1)}, f32[144]{0:T(256)}, u32[]{:S(2)}) copy-start(f32[144]{0:T(256)} %param.14) | copy-start | bytes 1732
  42.2 27.1 %copy-start.8 = (f32[144]{0:T(256)S(1)}, f32[144]{0:T(256)}, u32[]{:S(2)}) copy-start(f32[144]{0:T(256)} %param.15) | copy-start | bytes 1732
  69.7 8.9 %collective-permute-start.2 = (bf16[144,256]{1,0:T(8,128)(2,1)S(1)}, bf16[144,256]{1,0:T(8,128)(2,1)S(1)}, u32[]{:S(2)}, u32[]{:S(2)}) collective-permute-start(bf16[144,256]{1,0:T(8,128)(2,1)S(1)} %get-tuple-element.241), channel_id=1, source_target_pairs={{0,224},{1,160},{2,240},{3,96},{4,80},{5,112},{6,48},{7,64},{8,0},... | collective-permute-start | bytes 221192 | tf_op jit(solution)/shard_map/ppermute | solution.py:121
  103.5 3.9 %collective-permute-start.3 = (bf16[8,144,256]{2,1,0:T(8,128)(2,1)S(1)}, bf16[8,144,256]{2,1,0:T(8,128)(2,1)S(1)}, u32[]{:S(2)}, u32[]{:S(2)}) collective-permute-start(bf16[8,144,256]{2,1,0:T(8,128)(2,1)S(1)} %get-tuple-element.199), channel_id=1, source_target_pairs={{0,1},{1,0},{2,3},{3,2},{4,5},{5,4},{6,7},{7,6},{8,9},{9,8},{10,11... | collective-permute-start | bytes 1769480 | tf_op jit(solution)/shard_map/ppermute | solution.py:129

commit v3 on v2

--- a/solution.py
+++ b/solution.py
@@ -66,21 +66,23 @@
     )(stiff)
 
 
-def half_product(stiff, segment, swapped, dtype):
-    half, _, owned, depth = stiff.shape
+def class_product(stiff, segment, other_layer, other_core, dtype):
+    quarter, _, _, owned, depth = stiff.shape
     members = segment.shape[1]
 
     def kernel(stiff_ref, segment_ref, out_ref, kept_ref):
-        core = (lax.axis_index("col") + swapped) % 2
-        rows = stiff_ref[:, core].reshape(half * owned, depth)
+        col = lax.axis_index("col")
+        layer_parity = (col // 2 + other_layer) % 2
+        core = (col + other_core) % 2
+        rows = stiff_ref[:, layer_parity, core].reshape(quarter * owned, depth)
         product = jnp.dot(rows, segment_ref[...], preferred_element_type=jnp.float32)
-        out_ref[...] = product.reshape(half, owned, members).astype(dtype)
+        out_ref[...] = product.reshape(quarter, owned, members).astype(dtype)
 
     vmem = pl.BlockSpec(memory_space=pltpu.VMEM)
     return pl.pallas_call(
         kernel,
         out_shape=(
-            jax.ShapeDtypeStruct((half, owned, members), dtype),
+            jax.ShapeDtypeStruct((quarter, owned, members), dtype),
             jax.ShapeDtypeStruct(stiff.shape, stiff.dtype),
         ),
         in_specs=[vmem, vmem],
@@ -88,8 +90,8 @@
         input_output_aliases={0: 1},
         compiler_params=pltpu.CompilerParams(vmem_limit_bytes=VMEM_LIMIT),
         cost_estimate=pl.CostEstimate(
-            flops=2 * half * owned * depth * members,
-            bytes_accessed=2 * half * owned * depth,
+            flops=2 * quarter * owned * depth * members,
+            bytes_accessed=2 * quarter * owned * depth,
             transcendentals=0,
         ),
     )(stiff, segment)
@@ -111,9 +113,18 @@
     rows = landing_rows(side, 4)
     spread = [(a * side + b, rows[a][b] * side + a) for a in everyone for b in everyone]
     plane_groups = [[rows[a][b] * side + a for b in everyone] for a in everyone]
-    same_core = [[2 * z + core for z in range(layers)] for core in range(2)]
+    same_class = [
+        [2 * z + core for z in range(parity, layers, 2)]
+        for core in range(2)
+        for parity in range(2)
+    ]
     swap = [(c, c ^ 1) for c in everyone]
-    stiff = stiffness.reshape(layers, 2, owned, side * owned)
+    beside = []
+    for c in everyone:
+        z, core = c // 2, c % 2
+        ahead = (z + core) % 2 == 0
+        beside.append((c, 2 * ((z + (1 if ahead else -1)) % layers) + core))
+    stiff = stiffness.reshape(layers // 2, 2, 2, owned, side * owned)
     positions = first_patch + jnp.arange(owned, dtype=jnp.int32)
     depth = 0.5 + 1.5 * (positions.astype(jnp.float32) + 0.5) / patch_total
 
@@ -125,12 +136,17 @@
             copies, BOTH, 0, 0, axis_index_groups=plane_groups, tiled=True
         ).reshape(side * owned, members)
         segment, stiff, late = lax.optimization_barrier((segment, stiff, late))
-        away, stiff = half_product(stiff, segment, 1, jnp.bfloat16)
-        received = lax.ppermute(away, "col", swap)
-        own, stiff = half_product(stiff, segment, 0, jnp.float32)
-        kept = (own + received.astype(jnp.float32)).astype(jnp.bfloat16)
+        part, stiff = class_product(stiff, segment, 1, 1, jnp.float32)
+        received = lax.ppermute(part, "col", swap)
+        own, stiff = class_product(stiff, segment, 1, 0, jnp.float32)
+        onward = (own + received.astype(jnp.float32)).astype(jnp.bfloat16)
+        arrived = lax.ppermute(onward, "col", beside)
+        part, stiff = class_product(stiff, segment, 0, 1, jnp.float32)
+        received = lax.ppermute(part, "col", swap)
+        own, stiff = class_product(stiff, segment, 0, 0, jnp.float32)
+        kept = (own + received + arrived.astype(jnp.float32)).astype(jnp.bfloat16)
         kept, stiff, late = lax.optimization_barrier((kept, stiff, late))
-        terms = lax.all_to_all(kept, "col", 0, 0, axis_index_groups=same_core, tiled=True)
+        terms = lax.all_to_all(kept, "col", 0, 0, axis_index_groups=same_class, tiled=True)
         terms, stiff, late = lax.optimization_barrier((terms, stiff, late))
         return jnp.sum(terms.astype(jnp.float32), axis=0), stiff, late
 

time: 153 us -> 152 us (level)
  blocking collectives: 118 us -> 99.8 us
  starting transfers between devices: 14 us -> 22.2 us
  waiting for transfers between devices: 4.94 us -> 12.7 us
    all_to_all x2, blocking collectives: 48.6 us -> 29.5 us  [coupling(): lax.all_to_all(kept, 'col', 0, 0, axis_index_groups=same_class, tiled=True)]
    ppermute x2 -> x6, waiting for transfers between devices: 0.12 us -> 8.46 us  [the longest x2 8.23 us: coupling(): arrived = lax.ppermute(onward, 'col', beside)]
    ppermute x2 -> x6, starting transfers between devices: 3.05 us -> 10.8 us  [the longest x2 7.57 us: coupling(): arrived = lax.ppermute(onward, 'col', beside)]
    pallas_call x4 -> x8, Pallas kernels: 6.21 us -> 6.82 us  [class_product(): pl.pallas_call(kernel, out_shape=(jax.ShapeDtypeStruct((quarter, owned, m...]
  transfers between devices with their start and end apart: 4 -> 8, of which waited for: 3 -> 4; matrix products, arithmetic and copies ran while one was open for 0% -> 0% of each run, Pallas kernels for 3% -> 4%
where the time goes in v3:
time: 152 us; the launch traced here: 151 us
  blocking collectives  99.8 us (66%)
  starting transfers between devices  22.2 us (15%)
  waiting for transfers between devices  12.7 us (8%)
  Pallas kernels  7.71 us (5%)
  local copies, waits for them, and re-layouts  4.25 us (3%)
  other arithmetic  3.61 us (2%)
    all_to_all x2, blocking collectives, coupling(): lax.all_to_all(copies, BOTH, 0, 0, axis_index_groups=plane_groups, tiled=...  47.7 us
    all_to_all x2, blocking collectives, coupling(): lax.all_to_all(kept, 'col', 0, 0, axis_index_groups=same_class, tiled=True)  29.5 us
    all_to_all x2, blocking collectives, total_over(): return jnp.sum(lax.all_to_all(copies, axis, 0, 0, tiled=True), axis=0)  22.5 us
    ppermute x2, starting transfers between devices, coupling(): moved = lax.ppermute(sent_block, BOTH, spread)  11.4 us
    ppermute x2, waiting for transfers between devices, coupling(): arrived = lax.ppermute(onward, 'col', beside)  8.23 us
    ppermute x2, starting transfers between devices, coupling(): arrived = lax.ppermute(onward, 'col', beside)  7.57 us
    pallas_call x8, Pallas kernels, class_product(): pl.pallas_call(kernel, out_shape=(jax.ShapeDtypeStruct((quarter, owned, m...  6.82 us
    ppermute x2, waiting for transfers between devices, coupling(): moved = lax.ppermute(sent_block, BOTH, spread)  4.2 us
  transfers between devices with their start and end apart: 8, of which 4 were waited for; matrix products, arithmetic and copies ran while one was open for 0% of the time, Pallas kernels for 4%

profile of v3, /device:TPU:1, one launch (start us, length us, event | category | flops | bytes accessed | tf_op | source)
XLA Modules:
  0.0 151.2 jit_solution(3170588540550317299)
XLA Ops:
  0.6 1.1 fusion.19
  1.8 6.9 %collective-permute-start = (bf16[144,256]{1,0:T(8,128)(2,1)S(1)}, bf16[144,256]{1,0:T(8,128)(2,1)S(1)}, u32[]{:S(2)}, u32[]{:S(2)}) collective-permute-start(bf16[144,256]{1,0:T(8,128)(2,1)S(1)} %fusion.19), channel_id=1, source_target_pairs={{0,224},{1,160},{2,240},{3,96},{4,80},{5,112},{6,48},{7,64},{8,0},... | collective-permute-start | bytes 221192 | tf_op jit(solution)/shard_map/ppermute | solution.py:132
  8.6 0.0 copy-start
  8.6 4.0 %copy-done = bf16[2304,2304]{1,0:T(8,128)(2,1)S(1)} copy-done((bf16[2304,2304]{1,0:T(8,128)(2,1)S(1)}, bf16[2304,2304]{1,0:T(8,128)(2,1)}, u32[]{:S(2)}) %copy-start) | copy-done | bytes 10616856
  12.6 0.9 shard_map.112.stiff_ref
  13.5 0.0 collective-permute-done
  13.5 0.1 broadcast_in_dim.8
  13.6 24.3 %all_to_all.32 = bf16[16,144,256]{2,1,0:T(8,128)(2,1)S(1)} all-to-all(bf16[16,144,256]{2,1,0:T(8,128)(2,1)S(1)} %broadcast_in_dim.8), channel_id=1, replica_groups={{224,160,240,96,80,112,48,64,0,16,192,32,128,208,144,176},{177,241,113,..., dimensions={0} | all-to-all | bytes 2359296 | tf_op jit(solution)/shard_map/all_to_all | solution.py:135
  38.0 0.8 shard_map.113
  38.8 0.8 collective-permute-start.2
  39.6 0.9 shard_map.114
  40.5 0.9 shard_map.115
  41.3 0.0 copy-start.6
  41.4 0.0 copy-start.5
  41.4 0.0 copy-start.1
  41.4 0.0 copy-start.2
  41.4 0.0 copy-start.3
  41.4 0.0 copy-start.4
  41.4 0.0 copy-start.7
  41.4 0.0 copy-start.8
  41.4 0.1 collective-permute-start.1
  41.5 0.0 collective-permute-done.2
  41.6 0.1 add_convert_fusion.3
  41.7 6.8 %collective-permute-start.3 = (bf16[4,144,256]{2,1,0:T(8,128)(2,1)S(1)}, bf16[4,144,256]{2,1,0:T(8,128)(2,1)S(1)}, u32[]{:S(2)}, u32[]{:S(2)}) collective-permute-start(bf16[4,144,256]{2,1,0:T(8,128)(2,1)S(1)} %add_convert_fusion.3), channel_id=1, source_target_pairs={{0,2},{1,15},{2,0},{3,5},{4,6},{5,3},{6,4},{7,9},{8,10},{9,7},{10,... | collective-permute-start | bytes 884744 | tf_op jit(solution)/shard_map/ppermute | solution.py:143
  48.4 0.9 shard_map.116
  49.3 0.0 collective-permute-done.1
  49.3 3.2 %collective-permute-done.3 = bf16[4,144,256]{2,1,0:T(8,128)(2,1)S(1)} collective-permute-done((bf16[4,144,256]{2,1,0:T(8,128)(2,1)S(1)}, bf16[4,144,256]{2,1,0:T(8,128)(2,1)S(1)}, u32[]{:S(2)}, u32[]{:S(2)}) %collective-permute-start.3) | collective-permute-done | bytes 294944 | tf_op jit(solution)/shard_map/ppermute | solution.py:143
  52.5 0.1 add_convert_fusion.2
  52.7 14.7 %all_to_all.33 = bf16[4,144,256]{2,1,0:T(8,128)(2,1)S(1)} all-to-all(bf16[4,144,256]{2,1,0:T(8,128)(2,1)S(1)} %add_convert_fusion.2), channel_id=1, replica_groups={{0,4,8,12},{2,6,10,14},{1,5,9,13},{3,7,11,15},{16,20,24,28},{18,22,26,3..., dimensions={0} | all-to-all | bytes 589824 | tf_op jit(solution)/shard_map/all_to_all | solution.py:149
  67.3 0.0 copy-done.6
  67.4 0.0 copy-done.5
  67.4 0.0 copy-done.1
  67.4 0.0 copy-done.2
  67.4 0.0 copy-done.3
  67.4 0.0 copy-done.4
  67.4 0.0 copy-done.7
  67.4 0.0 copy-done.8
  67.4 0.4 fusion.18
  67.8 4.5 %collective-permute-start.4 = (bf16[144,256]{1,0:T(8,128)(2,1)S(1)}, bf16[144,256]{1,0:T(8,128)(2,1)S(1)}, u32[]{:S(2)}, u32[]{:S(2)}) collective-permute-start(bf16[144,256]{1,0:T(8,128)(2,1)S(1)} %get-tuple-element.257), channel_id=1, source_target_pairs={{0,224},{1,160},{2,240},{3,96},{4,80},{5,112},{6,48},{7,64},{8,0},... | collective-permute-start | bytes 221192 | tf_op jit(solution)/shard_map/ppermute | solution.py:132
  72.3 4.2 %collective-permute-done.4 = bf16[144,256]{1,0:T(8,128)(2,1)S(1)} collective-permute-done((bf16[144,256]{1,0:T(8,128)(2,1)S(1)}, bf16[144,256]{1,0:T(8,128)(2,1)S(1)}, u32[]{:S(2)}, u32[]{:S(2)}) %collective-permute-start.4) | collective-permute-done | bytes 73760 | tf_op jit(solution)/shard_map/ppermute | solution.py:132
  76.5 0.1 broadcast_in_dim.9
  76.6 23.4 %all_to_all.34 = bf16[16,144,256]{2,1,0:T(8,128)(2,1)S(1)} all-to-all(bf16[16,144,256]{2,1,0:T(8,128)(2,1)S(1)} %broadcast_in_dim.9), channel_id=1, replica_groups={{224,160,240,96,80,112,48,64,0,16,192,32,128,208,144,176},{177,241,113,..., dimensions={0} | all-to-all | bytes 2359296 | tf_op jit(solution)/shard_map/all_to_all | solution.py:135
  100.0 0.8 shard_map.117
  100.9 2.2 %collective-permute-start.6 = (f32[4,144,256]{2,1,0:T(8,128)S(1)}, f32[4,144,256]{2,1,0:T(8,128)S(1)}, u32[]{:S(2)}, u32[]{:S(2)}) collective-permute-start(f32[4,144,256]{2,1,0:T(8,128)S(1)} %get-tuple-element.215), channel_id=1, source_target_pairs={{0,1},{1,0},{2,3},{3,2},{4,5},{5,4},{6,7},{7,6},{8,9},{9,8},{10,11... | collective-permute-start | bytes 1769480 | tf_op jit(solution)/shard_map/ppermute | solution.py:140
  103.1 0.9 shard_map.118
  104.0 0.9 shard_map.119
  104.9 0.1 collective-permute-start.5
  105.0 0.0 collective-permute-done.6
  105.0 0.1 add_convert_fusion.1
  105.1 0.8 collective-permute-start.7
  105.9 0.9 shard_map.120
  106.7 0.2 collective-permute-done.5
  106.9 5.0 %collective-permute-done.7 = bf16[4,144,256]{2,1,0:T(8,128)(2,1)S(1)} collective-permute-done((bf16[4,144,256]{2,1,0:T(8,128)(2,1)S(1)}, bf16[4,144,256]{2,1,0:T(8,128)(2,1)S(1)}, u32[]{:S(2)}, u32[]{:S(2)}) %collective-permute-start.7) | collective-permute-done | bytes 294944 | tf_op jit(solution)/shard_map/ppermute | solution.py:143
  111.9 0.1 add_convert_fusion
  112.0 14.9 %all_to_all.35 = bf16[4,144,256]{2,1,0:T(8,128)(2,1)S(1)} all-to-all(bf16[4,144,256]{2,1,0:T(8,128)(2,1)S(1)} %add_convert_fusion), channel_id=1, replica_groups={{0,4,8,12},{2,6,10,14},{1,5,9,13},{3,7,11,15},{16,20,24,28},{18,22,26,3..., dimensions={0} | all-to-all | bytes 589824 | tf_op jit(solution)/shard_map/all_to_all | solution.py:149
  127.0 1.0 add_reduce_fusion
  128.0 11.8 %all_to_all.36 = f32[16,1,256]{2,1,0:T(1,128)S(1)} all-to-all(f32[16,1,256]{2,1,0:T(1,128)S(1)} %broadcast_in_dim.10), channel_id=1, replica_groups=mesh['row'=16,'col'=16] {'col'}, dimensions={0} | all-to-all | bytes 32768 | tf_op jit(solution)/shard_map/all_to_all | solution.py:165
  139.8 10.8 %all_to_all.37 = f32[16,1,256]{2,1,0:T(1,128)S(1)} all-to-all(f32[16,1,256]{2,1,0:T(1,128)S(1)} %broadcast_in_dim.11), channel_id=1, replica_groups=mesh['row'=16,'col'=16] {'row'}, dimensions={0} | all-to-all | bytes 32768 | tf_op jit(solution)/shard_map/all_to_all | solution.py:165
  150.6 0.6 sqrt_multiply_fusion
  (12 shorter events, 0.2 us)
Async XLA Ops:
  1.8 11.8 %collective-permute-start = (bf16[144,256]{1,0:T(8,128)(2,1)S(1)}, bf16[144,256]{1,0:T(8,128)(2,1)S(1)}, u32[]{:S(2)}, u32[]{:S(2)}) collective-permute-start(bf16[144,256]{1,0:T(8,128)(2,1)S(1)} %fusion.19), channel_id=1, source_target_pairs={{0,224},{1,160},{2,240},{3,96},{4,80},{5,112},{6,48},{7,64},{8,0},... | collective-permute-start | bytes 221192 | tf_op jit(solution)/shard_map/ppermute | solution.py:132
  8.6 4.0 %copy-start = (bf16[2304,2304]{1,0:T(8,128)(2,1)S(1)}, bf16[2304,2304]{1,0:T(8,128)(2,1)}, u32[]{:S(2)}) copy-start(bf16[2304,2304]{1,0:T(8,128)(2,1)} %param.9) | copy-start | bytes 31850500
  38.8 2.7 %collective-permute-start.2 = (f32[4,144,256]{2,1,0:T(8,128)S(1)}, f32[4,144,256]{2,1,0:T(8,128)S(1)}, u32[]{:S(2)}, u32[]{:S(2)}) collective-permute-start(f32[4,144,256]{2,1,0:T(8,128)S(1)} %get-tuple-element.153), channel_id=1, source_target_pairs={{0,1},{1,0},{2,3},{3,2},{4,5},{5,4},{6,7},{7,6},{8,9},{9,8},{10,11... | collective-permute-start | bytes 1769480 | tf_op jit(solution)/shard_map/ppermute | solution.py:140
  41.3 26.0 %copy-start.6 = (f32[144]{0:T(256)S(1)}, f32[144]{0:T(256)}, u32[]{:S(2)}) copy-start(f32[144]{0:T(256)} %param.10) | copy-start | bytes 1732
  41.4 26.0 %copy-start.5 = (f32[144]{0:T(256)S(1)}, f32[144]{0:T(256)}, u32[]{:S(2)}) copy-start(f32[144]{0:T(256)} %param.16) | copy-start | bytes 1732
  41.4 26.0 %copy-start.1 = (f32[144,256]{1,0:T(8,128)S(1)}, f32[144,256]{1,0:T(8,128)}, u32[]{:S(2)}) copy-start(f32[144,256]{1,0:T(8,128)} %param.11) | copy-start | bytes 442372
  41.4 26.0 %copy-start.2 = (f32[144,256]{1,0:T(8,128)S(1)}, f32[144,256]{1,0:T(8,128)}, u32[]{:S(2)}) copy-start(f32[144,256]{1,0:T(8,128)} %param.12) | copy-start | bytes 442372
  41.4 26.0 %copy-start.3 = (f32[144]{0:T(256)S(1)}, f32[144]{0:T(256)}, u32[]{:S(2)}) copy-start(f32[144]{0:T(256)} %param.13) | copy-start | bytes 1732
  41.4 26.0 %copy-start.4 = (f32[256]{0:T(256)S(1)}, f32[256]{0:T(256)}, u32[]{:S(2)}) copy-start(f32[256]{0:T(256)} %param.17) | copy-start | bytes 3076
  41.4 26.0 %copy-start.7 = (f32[144]{0:T(256)S(1)}, f32[144]{0:T(256)}, u32[]{:S(2)}) copy-start(f32[144]{0:T(256)} %param.14) | copy-start | bytes 1732
  41.4 26.0 %copy-start.8 = (f32[144]{0:T(256)S(1)}, f32[144]{0:T(256)}, u32[]{:S(2)}) copy-start(f32[144]{0:T(256)} %param.15) | copy-start | bytes 1732
  41.4 7.9 %collective-permute-start.1 = (f32[4,144,256]{2,1,0:T(8,128)S(1)}, f32[4,144,256]{2,1,0:T(8,128)S(1)}, u32[]{:S(2)}, u32[]{:S(2)}) collective-permute-start(f32[4,144,256]{2,1,0:T(8,128)S(1)} %get-tuple-element.151), channel_id=1, source_target_pairs={{0,1},{1,0},{2,3},{3,2},{4,5},{5,4},{6,7},{7,6},{8,9},{9,8},{10,11... | collective-permute-start | bytes 1769480 | tf_op jit(solution)/shard_map/ppermute | solution.py:145
  41.7 10.9 %collective-permute-start.3 = (bf16[4,144,256]{2,1,0:T(8,128)(2,1)S(1)}, bf16[4,144,256]{2,1,0:T(8,128)(2,1)S(1)}, u32[]{:S(2)}, u32[]{:S(2)}) collective-permute-start(bf16[4,144,256]{2,1,0:T(8,128)(2,1)S(1)} %add_convert_fusion.3), channel_id=1, source_target_pairs={{0,2},{1,15},{2,0},{3,5},{4,6},{5,3},{6,4},{7,9},{8,10},{9,7},{10,... | collective-permute-start | bytes 884744 | tf_op jit(solution)/shard_map/ppermute | solution.py:143
  67.8 8.7 %collective-permute-start.4 = (bf16[144,256]{1,0:T(8,128)(2,1)S(1)}, bf16[144,256]{1,0:T(8,128)(2,1)S(1)}, u32[]{:S(2)}, u32[]{:S(2)}) collective-permute-start(bf16[144,256]{1,0:T(8,128)(2,1)S(1)} %get-tuple-element.257), channel_id=1, source_target_pairs={{0,224},{1,160},{2,240},{3,96},{4,80},{5,112},{6,48},{7,64},{8,0},... | collective-permute-start | bytes 221192 | tf_op jit(solution)/shard_map/ppermute | solution.py:132
  100.9 4.1 %collective-permute-start.6 = (f32[4,144,256]{2,1,0:T(8,128)S(1)}, f32[4,144,256]{2,1,0:T(8,128)S(1)}, u32[]{:S(2)}, u32[]{:S(2)}) collective-permute-start(f32[4,144,256]{2,1,0:T(8,128)S(1)} %get-tuple-element.215), channel_id=1, source_target_pairs={{0,1},{1,0},{2,3},{3,2},{4,5},{5,4},{6,7},{7,6},{8,9},{9,8},{10,11... | collective-permute-start | bytes 1769480 | tf_op jit(solution)/shard_map/ppermute | solution.py:140
  104.9 2.1 %collective-permute-start.5 = (f32[4,144,256]{2,1,0:T(8,128)S(1)}, f32[4,144,256]{2,1,0:T(8,128)S(1)}, u32[]{:S(2)}, u32[]{:S(2)}) collective-permute-start(f32[4,144,256]{2,1,0:T(8,128)S(1)} %get-tuple-element.213), channel_id=1, source_target_pairs={{0,1},{1,0},{2,3},{3,2},{4,5},{5,4},{6,7},{7,6},{8,9},{9,8},{10,11... | collective-permute-start | bytes 1769480 | tf_op jit(solution)/shard_map/ppermute | solution.py:145
  105.1 6.9 %collective-permute-start.7 = (bf16[4,144,256]{2,1,0:T(8,128)(2,1)S(1)}, bf16[4,144,256]{2,1,0:T(8,128)(2,1)S(1)}, u32[]{:S(2)}, u32[]{:S(2)}) collective-permute-start(bf16[4,144,256]{2,1,0:T(8,128)(2,1)S(1)} %add_convert_fusion.1), channel_id=1, source_target_pairs={{0,2},{1,15},{2,0},{3,5},{4,6},{5,3},{6,4},{7,9},{8,10},{9,7},{10,... | collective-permute-start | bytes 884744 | tf_op jit(solution)/shard_map/ppermute | solution.py:143

commit v4 on v3

--- a/solution.py
+++ b/solution.py
@@ -97,6 +97,28 @@
     )(stiff, segment)
 
 
+def dealt(own, received, arrived):
+    quarter, owned, members = own.shape
+
+    def kernel(own_ref, received_ref, arrived_ref, *out_refs):
+        place = lax.axis_index("col") // 4
+        for distance, out_ref in enumerate(out_refs):
+            chunk = (place + distance) % quarter
+            total = own_ref[chunk] + received_ref[chunk]
+            total = total + arrived_ref[chunk].astype(jnp.float32)
+            out_ref[...] = total.astype(out_ref.dtype)
+
+    vmem = pl.BlockSpec(memory_space=pltpu.VMEM)
+    types = [jnp.float32] + [jnp.bfloat16] * (quarter - 1)
+    return pl.pallas_call(
+        kernel,
+        out_shape=[jax.ShapeDtypeStruct((owned, members), t) for t in types],
+        in_specs=[vmem] * 3,
+        out_specs=[vmem] * quarter,
+        compiler_params=pltpu.CompilerParams(vmem_limit_bytes=VMEM_LIMIT),
+    )(own, received, arrived)
+
+
 def body(
     stiffness, self_stiffness, stress, state, plate_rate, stress_gain, heal_rate, ab_ratio, step
 ):
@@ -113,11 +135,7 @@
     rows = landing_rows(side, 4)
     spread = [(a * side + b, rows[a][b] * side + a) for a in everyone for b in everyone]
     plane_groups = [[rows[a][b] * side + a for b in everyone] for a in everyone]
-    same_class = [
-        [2 * z + core for z in range(parity, layers, 2)]
-        for core in range(2)
-        for parity in range(2)
-    ]
+    along = [[(c, (c + 4 * d) % side) for c in everyone] for d in range(layers // 2)]
     swap = [(c, c ^ 1) for c in everyone]
     beside = []
     for c in everyone:
@@ -144,11 +162,14 @@
         part, stiff = class_product(stiff, segment, 0, 1, jnp.float32)
         received = lax.ppermute(part, "col", swap)
         own, stiff = class_product(stiff, segment, 0, 0, jnp.float32)
-        kept = (own + received + arrived.astype(jnp.float32)).astype(jnp.bfloat16)
-        kept, stiff, late = lax.optimization_barrier((kept, stiff, late))
-        terms = lax.all_to_all(kept, "col", 0, 0, axis_index_groups=same_class, tiled=True)
-        terms, stiff, late = lax.optimization_barrier((terms, stiff, late))
-        return jnp.sum(terms.astype(jnp.float32), axis=0), stiff, late
+        held, *sent = dealt(own, received, arrived)
+        held, sent, stiff, late = lax.optimization_barrier((held, sent, stiff, late))
+        coupled = held
+        for distance in (2, 1, 3):
+            chunk = lax.ppermute(sent[distance - 1], "col", along[distance])
+            coupled = coupled + chunk.astype(jnp.float32)
+        coupled, stiff, late = lax.optimization_barrier((coupled, stiff, late))
+        return coupled, stiff, late
 
     def section(stress_now, state_now, stiff, late):
         params = late[:5]

time: 152 us -> 147 us (0.967)
  blocking collectives: 99.8 us -> 70.7 us
  starting transfers between devices: 22.2 us -> 42 us
  waiting for transfers between devices: 12.7 us -> 18 us
    all_to_all x2 -> x0, blocking collectives: 29.5 us -> none  [coupling(): lax.all_to_all(kept, 'col', 0, 0, axis_index_groups=same_class, tiled=True)]
    ppermute x0 -> x6, starting transfers between devices: none -> 14.9 us  [coupling(): chunk = lax.ppermute(sent[distance - 1], 'col', along[distance])]
    ppermute x0 -> x6, waiting for transfers between devices: none -> 7.51 us  [coupling(): chunk = lax.ppermute(sent[distance - 1], 'col', along[distance])]
    ppermute x2, starting transfers between devices: 7.57 us -> 11.9 us  [coupling(): arrived = lax.ppermute(onward, 'col', beside)]
    ppermute x2, waiting for transfers between devices: 8.23 us -> 6.48 us  [coupling(): arrived = lax.ppermute(onward, 'col', beside)]
  transfers between devices with their start and end apart: 8 -> 14, of which waited for: 4 -> 8; matrix products, arithmetic and copies ran while one was open for 0% -> 0% of each run, Pallas kernels for 4% -> 4%
where the time goes in v4:
time: 147 us
  blocking collectives  70.7 us (48%)
  starting transfers between devices  42 us (29%)
  waiting for transfers between devices  18 us (12%)
  Pallas kernels  7.89 us (5%)
  local copies, waits for them, and re-layouts  4.25 us (3%)
  other arithmetic  3.48 us (2%)
    all_to_all x2, blocking collectives, coupling(): lax.all_to_all(copies, BOTH, 0, 0, axis_index_groups=plane_groups, tiled=...  47.9 us
    all_to_all x2, blocking collectives, total_over(): return jnp.sum(lax.all_to_all(copies, axis, 0, 0, tiled=True), axis=0)  22.7 us
    ppermute x6, starting transfers between devices, coupling(): chunk = lax.ppermute(sent[distance - 1], 'col', along[distance])  14.9 us
    ppermute x2, starting transfers between devices, coupling(): arrived = lax.ppermute(onward, 'col', beside)  11.9 us
    ppermute x2, starting transfers between devices, coupling(): moved = lax.ppermute(sent_block, BOTH, spread)  11.8 us
    ppermute x6, waiting for transfers between devices, coupling(): chunk = lax.ppermute(sent[distance - 1], 'col', along[distance])  7.51 us
    pallas_call x8, Pallas kernels, class_product(): pl.pallas_call(kernel, out_shape=(jax.ShapeDtypeStruct((quarter, owned, m...  6.82 us
    ppermute x2, waiting for transfers between devices, coupling(): arrived = lax.ppermute(onward, 'col', beside)  6.48 us
  transfers between devices with their start and end apart: 14, of which 8 were waited for; matrix products, arithmetic and copies ran while one was open for 0% of the time, Pallas kernels for 4%

profile of v4, /device:TPU:1, one launch (start us, length us, event | category | flops | bytes accessed | tf_op | source)
XLA Modules:
  0.0 147.2 jit_solution(5685926340362570052)
XLA Ops:
  0.6 1.1 fusion.19
  1.8 6.9 %collective-permute-start = (bf16[144,256]{1,0:T(8,128)(2,1)S(1)}, bf16[144,256]{1,0:T(8,128)(2,1)S(1)}, u32[]{:S(2)}, u32[]{:S(2)}) collective-permute-start(bf16[144,256]{1,0:T(8,128)(2,1)S(1)} %fusion.19), channel_id=1, source_target_pairs={{0,224},{1,160},{2,240},{3,96},{4,80},{5,112},{6,48},{7,64},{8,0},... | collective-permute-start | bytes 221192 | tf_op jit(solution)/shard_map/ppermute | solution.py:150
  8.6 4.0 %copy-done = bf16[2304,2304]{1,0:T(8,128)(2,1)S(1)} copy-done((bf16[2304,2304]{1,0:T(8,128)(2,1)S(1)}, bf16[2304,2304]{1,0:T(8,128)(2,1)}, u32[]{:S(2)}) %copy-start) | copy-done | bytes 10616856
  12.6 0.9 shard_map.112.stiff_ref
  13.5 0.0 collective-permute-done
  13.5 0.1 broadcast_in_dim.8
  13.6 24.3 %all_to_all.22 = bf16[16,144,256]{2,1,0:T(8,128)(2,1)S(1)} all-to-all(bf16[16,144,256]{2,1,0:T(8,128)(2,1)S(1)} %broadcast_in_dim.8), channel_id=1, replica_groups={{224,160,240,96,80,112,48,64,0,16,192,32,128,208,144,176},{177,241,113,..., dimensions={0} | all-to-all | bytes 2359296 | tf_op jit(solution)/shard_map/all_to_all | solution.py:153
  38.0 0.9 shard_map.113
  38.8 0.8 collective-permute-start.2
  39.6 0.9 shard_map.114
  40.5 0.0 copy-start.5
  40.5 0.0 copy-start.6
  40.5 0.0 copy-start.1
  40.5 0.0 copy-start.2
  40.5 0.0 copy-start.3
  40.6 0.0 copy-start.4
  40.6 0.0 copy-start.7
  40.6 0.0 copy-start.8
  40.6 0.9 shard_map.115
  41.4 0.1 collective-permute-start.1
  41.6 0.0 collective-permute-done.2
  41.6 0.1 add_convert_fusion.1
  41.7 6.8 %collective-permute-start.3 = (bf16[4,144,256]{2,1,0:T(8,128)(2,1)S(1)}, bf16[4,144,256]{2,1,0:T(8,128)(2,1)S(1)}, u32[]{:S(2)}, u32[]{:S(2)}) collective-permute-start(bf16[4,144,256]{2,1,0:T(8,128)(2,1)S(1)} %add_convert_fusion.1), channel_id=1, source_target_pairs={{0,2},{1,15},{2,0},{3,5},{4,6},{5,3},{6,4},{7,9},{8,10},{9,7},{10,... | collective-permute-start | bytes 884744 | tf_op jit(solution)/shard_map/ppermute | solution.py:161
  48.5 0.9 shard_map.116
  49.3 0.0 collective-permute-done.1.received_ref
  49.3 3.2 %collective-permute-done.3.arrived_ref = bf16[4,144,256]{2,1,0:T(8,128)(2,1)S(1)} collective-permute-done((bf16[4,144,256]{2,1,0:T(8,128)(2,1)S(1)}, bf16[4,144,256]{2,1,0:T(8,128)(2,1)S(1)}, u32[]{:S(2)}, u32[]{:S(2)}) %collective-permute-start.3) | collective-permute-done | bytes 294944 | tf_op jit(solution)/shard_map/ppermute | solution.py:161
  52.6 0.1 shard_map.117
  52.7 3.4 %collective-permute-start.4 = (bf16[144,256]{1,0:T(8,128)(2,1)S(1)}, bf16[144,256]{1,0:T(8,128)(2,1)S(1)}, u32[]{:S(2)}, u32[]{:S(2)}) collective-permute-start(bf16[144,256]{1,0:T(8,128)(2,1)S(1)} %get-tuple-element.185), channel_id=1, source_target_pairs={{0,8},{1,9},{2,10},{3,11},{4,12},{5,13},{6,14},{7,15},{8,0},{9,1},... | collective-permute-start | bytes 221192 | tf_op jit(solution)/shard_map/ppermute | solution.py:169
  56.1 0.1 collective-permute-start.5
  56.2 3.4 %collective-permute-start.6 = (bf16[144,256]{1,0:T(8,128)(2,1)S(1)}, bf16[144,256]{1,0:T(8,128)(2,1)S(1)}, u32[]{:S(2)}, u32[]{:S(2)}) collective-permute-start(bf16[144,256]{1,0:T(8,128)(2,1)S(1)} %get-tuple-element.187), channel_id=1, source_target_pairs={{0,12},{1,13},{2,14},{3,15},{4,0},{5,1},{6,2},{7,3},{8,4},{9,5},{1... | collective-permute-start | bytes 221192 | tf_op jit(solution)/shard_map/ppermute | solution.py:169
  59.7 0.3 collective-permute-done.4
  60.0 1.6 %collective-permute-done.5 = bf16[144,256]{1,0:T(8,128)(2,1)S(1)} collective-permute-done((bf16[144,256]{1,0:T(8,128)(2,1)S(1)}, bf16[144,256]{1,0:T(8,128)(2,1)S(1)}, u32[]{:S(2)}, u32[]{:S(2)}) %collective-permute-start.5) | collective-permute-done | bytes 73760 | tf_op jit(solution)/shard_map/ppermute | solution.py:169
  61.5 0.3 collective-permute-done.6
  61.9 0.0 copy-done.1
  61.9 0.0 copy-done.2
  61.9 0.0 copy-done.3
  61.9 0.0 copy-done.4
  62.0 0.4 fusion.18
  62.3 4.9 %collective-permute-start.7 = (bf16[144,256]{1,0:T(8,128)(2,1)S(1)}, bf16[144,256]{1,0:T(8,128)(2,1)S(1)}, u32[]{:S(2)}, u32[]{:S(2)}) collective-permute-start(bf16[144,256]{1,0:T(8,128)(2,1)S(1)} %get-tuple-element.285), channel_id=1, source_target_pairs={{0,224},{1,160},{2,240},{3,96},{4,80},{5,112},{6,48},{7,64},{8,0},... | collective-permute-start | bytes 221192 | tf_op jit(solution)/shard_map/ppermute | solution.py:150
  67.2 4.0 %collective-permute-done.7 = bf16[144,256]{1,0:T(8,128)(2,1)S(1)} collective-permute-done((bf16[144,256]{1,0:T(8,128)(2,1)S(1)}, bf16[144,256]{1,0:T(8,128)(2,1)S(1)}, u32[]{:S(2)}, u32[]{:S(2)}) %collective-permute-start.7) | collective-permute-done | bytes 73760 | tf_op jit(solution)/shard_map/ppermute | solution.py:150
  71.2 0.1 broadcast_in_dim.9
  71.3 23.6 %all_to_all.23 = bf16[16,144,256]{2,1,0:T(8,128)(2,1)S(1)} all-to-all(bf16[16,144,256]{2,1,0:T(8,128)(2,1)S(1)} %broadcast_in_dim.9), channel_id=1, replica_groups={{224,160,240,96,80,112,48,64,0,16,192,32,128,208,144,176},{177,241,113,..., dimensions={0} | all-to-all | bytes 2359296 | tf_op jit(solution)/shard_map/all_to_all | solution.py:153
  94.9 0.8 shard_map.118
  95.8 2.2 %collective-permute-start.9 = (f32[4,144,256]{2,1,0:T(8,128)S(1)}, f32[4,144,256]{2,1,0:T(8,128)S(1)}, u32[]{:S(2)}, u32[]{:S(2)}) collective-permute-start(f32[4,144,256]{2,1,0:T(8,128)S(1)} %get-tuple-element.236), channel_id=1, source_target_pairs={{0,1},{1,0},{2,3},{3,2},{4,5},{5,4},{6,7},{7,6},{8,9},{9,8},{10,11... | collective-permute-start | bytes 1769480 | tf_op jit(solution)/shard_map/ppermute | solution.py:158
  98.0 0.9 shard_map.119
  98.9 0.9 shard_map.120
  99.7 0.3 collective-permute-start.8
  100.0 0.0 collective-permute-done.9
  100.0 0.1 add_convert_fusion
  100.1 5.1 %collective-permute-start.10 = (bf16[4,144,256]{2,1,0:T(8,128)(2,1)S(1)}, bf16[4,144,256]{2,1,0:T(8,128)(2,1)S(1)}, u32[]{:S(2)}, u32[]{:S(2)}) collective-permute-start(bf16[4,144,256]{2,1,0:T(8,128)(2,1)S(1)} %add_convert_fusion), channel_id=1, source_target_pairs={{0,2},{1,15},{2,0},{3,5},{4,6},{5,3},{6,4},{7,9},{8,10},{9,7},{10,... | collective-permute-start | bytes 884744 | tf_op jit(solution)/shard_map/ppermute | solution.py:161
  105.3 0.9 shard_map.121
  106.1 0.0 collective-permute-done.8.received_ref
  106.1 3.2 %collective-permute-done.10.arrived_ref = bf16[4,144,256]{2,1,0:T(8,128)(2,1)S(1)} collective-permute-done((bf16[4,144,256]{2,1,0:T(8,128)(2,1)S(1)}, bf16[4,144,256]{2,1,0:T(8,128)(2,1)S(1)}, u32[]{:S(2)}, u32[]{:S(2)}) %collective-permute-start.10) | collective-permute-done | bytes 294944 | tf_op jit(solution)/shard_map/ppermute | solution.py:161
  109.4 0.1 shard_map.122
  109.5 4.3 %collective-permute-start.11 = (bf16[144,256]{1,0:T(8,128)(2,1)S(1)}, bf16[144,256]{1,0:T(8,128)(2,1)S(1)}, u32[]{:S(2)}, u32[]{:S(2)}) collective-permute-start(bf16[144,256]{1,0:T(8,128)(2,1)S(1)} %get-tuple-element.255), channel_id=1, source_target_pairs={{0,8},{1,9},{2,10},{3,11},{4,12},{5,13},{6,14},{7,15},{8,0},{9,1},... | collective-permute-start | bytes 221192 | tf_op jit(solution)/shard_map/ppermute | solution.py:169
  113.8 0.0 collective-permute-start.12
  113.8 3.6 %collective-permute-start.13 = (bf16[144,256]{1,0:T(8,128)(2,1)S(1)}, bf16[144,256]{1,0:T(8,128)(2,1)S(1)}, u32[]{:S(2)}, u32[]{:S(2)}) collective-permute-start(bf16[144,256]{1,0:T(8,128)(2,1)S(1)} %get-tuple-element.257), channel_id=1, source_target_pairs={{0,12},{1,13},{2,14},{3,15},{4,0},{5,1},{6,2},{7,3},{8,4},{9,5},{1... | collective-permute-start | bytes 221192 | tf_op jit(solution)/shard_map/ppermute | solution.py:169
  117.4 0.0 collective-permute-done.11
  117.4 3.5 %collective-permute-done.12 = bf16[144,256]{1,0:T(8,128)(2,1)S(1)} collective-permute-done((bf16[144,256]{1,0:T(8,128)(2,1)S(1)}, bf16[144,256]{1,0:T(8,128)(2,1)S(1)}, u32[]{:S(2)}, u32[]{:S(2)}) %collective-permute-start.12) | collective-permute-done | bytes 73760 | tf_op jit(solution)/shard_map/ppermute | solution.py:169
  120.8 1.9 %collective-permute-done.13 = bf16[144,256]{1,0:T(8,128)(2,1)S(1)} collective-permute-done((bf16[144,256]{1,0:T(8,128)(2,1)S(1)}, bf16[144,256]{1,0:T(8,128)(2,1)S(1)}, u32[]{:S(2)}, u32[]{:S(2)}) %collective-permute-start.13) | collective-permute-done | bytes 73760 | tf_op jit(solution)/shard_map/ppermute | solution.py:169
  122.8 1.0 add_reduce_fusion
  123.8 12.0 %all_to_all.24 = f32[16,1,256]{2,1,0:T(1,128)S(1)} all-to-all(f32[16,1,256]{2,1,0:T(1,128)S(1)} %broadcast_in_dim.10), channel_id=1, replica_groups=mesh['row'=16,'col'=16] {'col'}, dimensions={0} | all-to-all | bytes 32768 | tf_op jit(solution)/shard_map/all_to_all | solution.py:186
  135.8 10.8 %all_to_all.25 = f32[16,1,256]{2,1,0:T(1,128)S(1)} all-to-all(f32[16,1,256]{2,1,0:T(1,128)S(1)} %broadcast_in_dim.11), channel_id=1, replica_groups=mesh['row'=16,'col'=16] {'row'}, dimensions={0} | all-to-all | bytes 32768 | tf_op jit(solution)/shard_map/all_to_all | solution.py:186
  146.6 0.6 sqrt_multiply_fusion
  (17 shorter events, 0.2 us)
Async XLA Ops:
  1.8 11.8 %collective-permute-start = (bf16[144,256]{1,0:T(8,128)(2,1)S(1)}, bf16[144,256]{1,0:T(8,128)(2,1)S(1)}, u32[]{:S(2)}, u32[]{:S(2)}) collective-permute-start(bf16[144,256]{1,0:T(8,128)(2,1)S(1)} %fusion.19), channel_id=1, source_target_pairs={{0,224},{1,160},{2,240},{3,96},{4,80},{5,112},{6,48},{7,64},{8,0},... | collective-permute-start | bytes 221192 | tf_op jit(solution)/shard_map/ppermute | solution.py:150
  8.6 4.0 %copy-start = (bf16[2304,2304]{1,0:T(8,128)(2,1)S(1)}, bf16[2304,2304]{1,0:T(8,128)(2,1)}, u32[]{:S(2)}) copy-start(bf16[2304,2304]{1,0:T(8,128)(2,1)} %param.9) | copy-start | bytes 31850500
  38.8 2.7 %collective-permute-start.2 = (f32[4,144,256]{2,1,0:T(8,128)S(1)}, f32[4,144,256]{2,1,0:T(8,128)S(1)}, u32[]{:S(2)}, u32[]{:S(2)}) collective-permute-start(f32[4,144,256]{2,1,0:T(8,128)S(1)} %get-tuple-element.167), channel_id=1, source_target_pairs={{0,1},{1,0},{2,3},{3,2},{4,5},{5,4},{6,7},{7,6},{8,9},{9,8},{10,11... | collective-permute-start | bytes 1769480 | tf_op jit(solution)/shard_map/ppermute | solution.py:158
  40.5 21.4 %copy-start.5 = (f32[144]{0:T(256)S(1)}, f32[144]{0:T(256)}, u32[]{:S(2)}) copy-start(f32[144]{0:T(256)} %param.10) | copy-start | bytes 1732
  40.5 21.4 %copy-start.6 = (f32[144]{0:T(256)S(1)}, f32[144]{0:T(256)}, u32[]{:S(2)}) copy-start(f32[144]{0:T(256)} %param.16) | copy-start | bytes 1732
  40.5 21.4 %copy-start.1 = (f32[144,256]{1,0:T(8,128)S(1)}, f32[144,256]{1,0:T(8,128)}, u32[]{:S(2)}) copy-start(f32[144,256]{1,0:T(8,128)} %param.11) | copy-start | bytes 442372
  40.5 21.4 %copy-start.2 = (f32[144,256]{1,0:T(8,128)S(1)}, f32[144,256]{1,0:T(8,128)}, u32[]{:S(2)}) copy-start(f32[144,256]{1,0:T(8,128)} %param.12) | copy-start | bytes 442372
  40.5 21.4 %copy-start.3 = (f32[144]{0:T(256)S(1)}, f32[144]{0:T(256)}, u32[]{:S(2)}) copy-start(f32[144]{0:T(256)} %param.13) | copy-start | bytes 1732
  40.6 21.4 %copy-start.4 = (f32[256]{0:T(256)S(1)}, f32[256]{0:T(256)}, u32[]{:S(2)}) copy-start(f32[256]{0:T(256)} %param.17) | copy-start | bytes 3076
  40.6 21.4 %copy-start.7 = (f32[144]{0:T(256)S(1)}, f32[144]{0:T(256)}, u32[]{:S(2)}) copy-start(f32[144]{0:T(256)} %param.14) | copy-start | bytes 1732
  40.6 21.4 %copy-start.8 = (f32[144]{0:T(256)S(1)}, f32[144]{0:T(256)}, u32[]{:S(2)}) copy-start(f32[144]{0:T(256)} %param.15) | copy-start | bytes 1732
  41.4 7.9 %collective-permute-start.1 = (f32[4,144,256]{2,1,0:T(8,128)S(1)}, f32[4,144,256]{2,1,0:T(8,128)S(1)}, u32[]{:S(2)}, u32[]{:S(2)}) collective-permute-start(f32[4,144,256]{2,1,0:T(8,128)S(1)} %get-tuple-element.165), channel_id=1, source_target_pairs={{0,1},{1,0},{2,3},{3,2},{4,5},{5,4},{6,7},{7,6},{8,9},{9,8},{10,11... | collective-permute-start | bytes 1769480 | tf_op jit(solution)/shard_map/ppermute | solution.py:163
  41.7 10.9 %collective-permute-start.3 = (bf16[4,144,256]{2,1,0:T(8,128)(2,1)S(1)}, bf16[4,144,256]{2,1,0:T(8,128)(2,1)S(1)}, u32[]{:S(2)}, u32[]{:S(2)}) collective-permute-start(bf16[4,144,256]{2,1,0:T(8,128)(2,1)S(1)} %add_convert_fusion.1), channel_id=1, source_target_pairs={{0,2},{1,15},{2,0},{3,5},{4,6},{5,3},{6,4},{7,9},{8,10},{9,7},{10,... | collective-permute-start | bytes 884744 | tf_op jit(solution)/shard_map/ppermute | solution.py:161
  52.7 7.3 %collective-permute-start.4 = (bf16[144,256]{1,0:T(8,128)(2,1)S(1)}, bf16[144,256]{1,0:T(8,128)(2,1)S(1)}, u32[]{:S(2)}, u32[]{:S(2)}) collective-permute-start(bf16[144,256]{1,0:T(8,128)(2,1)S(1)} %get-tuple-element.185), channel_id=1, source_target_pairs={{0,8},{1,9},{2,10},{3,11},{4,12},{5,13},{6,14},{7,15},{8,0},{9,1},... | collective-permute-start | bytes 221192 | tf_op jit(solution)/shard_map/ppermute | solution.py:169
  56.1 5.5 %collective-permute-start.5 = (bf16[144,256]{1,0:T(8,128)(2,1)S(1)}, bf16[144,256]{1,0:T(8,128)(2,1)S(1)}, u32[]{:S(2)}, u32[]{:S(2)}) collective-permute-start(bf16[144,256]{1,0:T(8,128)(2,1)S(1)} %get-tuple-element.186), channel_id=1, source_target_pairs={{0,4},{1,5},{2,6},{3,7},{4,8},{5,9},{6,10},{7,11},{8,12},{9,13},{1... | collective-permute-start | bytes 221192 | tf_op jit(solution)/shard_map/ppermute | solution.py:169
  56.2 5.6 %collective-permute-start.6 = (bf16[144,256]{1,0:T(8,128)(2,1)S(1)}, bf16[144,256]{1,0:T(8,128)(2,1)S(1)}, u32[]{:S(2)}, u32[]{:S(2)}) collective-permute-start(bf16[144,256]{1,0:T(8,128)(2,1)S(1)} %get-tuple-element.187), channel_id=1, source_target_pairs={{0,12},{1,13},{2,14},{3,15},{4,0},{5,1},{6,2},{7,3},{8,4},{9,5},{1... | collective-permute-start | bytes 221192 | tf_op jit(solution)/shard_map/ppermute | solution.py:169
  62.3 8.9 %collective-permute-start.7 = (bf16[144,256]{1,0:T(8,128)(2,1)S(1)}, bf16[144,256]{1,0:T(8,128)(2,1)S(1)}, u32[]{:S(2)}, u32[]{:S(2)}) collective-permute-start(bf16[144,256]{1,0:T(8,128)(2,1)S(1)} %get-tuple-element.285), channel_id=1, source_target_pairs={{0,224},{1,160},{2,240},{3,96},{4,80},{5,112},{6,48},{7,64},{8,0},... | collective-permute-start | bytes 221192 | tf_op jit(solution)/shard_map/ppermute | solution.py:150
  95.8 4.2 %collective-permute-start.9 = (f32[4,144,256]{2,1,0:T(8,128)S(1)}, f32[4,144,256]{2,1,0:T(8,128)S(1)}, u32[]{:S(2)}, u32[]{:S(2)}) collective-permute-start(f32[4,144,256]{2,1,0:T(8,128)S(1)} %get-tuple-element.236), channel_id=1, source_target_pairs={{0,1},{1,0},{2,3},{3,2},{4,5},{5,4},{6,7},{7,6},{8,9},{9,8},{10,11... | collective-permute-start | bytes 1769480 | tf_op jit(solution)/shard_map/ppermute | solution.py:158
  99.7 6.4 %collective-permute-start.8 = (f32[4,144,256]{2,1,0:T(8,128)S(1)}, f32[4,144,256]{2,1,0:T(8,128)S(1)}, u32[]{:S(2)}, u32[]{:S(2)}) collective-permute-start(f32[4,144,256]{2,1,0:T(8,128)S(1)} %get-tuple-element.234), channel_id=1, source_target_pairs={{0,1},{1,0},{2,3},{3,2},{4,5},{5,4},{6,7},{7,6},{8,9},{9,8},{10,11... | collective-permute-start | bytes 1769480 | tf_op jit(solution)/shard_map/ppermute | solution.py:163
  100.1 9.3 %collective-permute-start.10 = (bf16[4,144,256]{2,1,0:T(8,128)(2,1)S(1)}, bf16[4,144,256]{2,1,0:T(8,128)(2,1)S(1)}, u32[]{:S(2)}, u32[]{:S(2)}) collective-permute-start(bf16[4,144,256]{2,1,0:T(8,128)(2,1)S(1)} %add_convert_fusion), channel_id=1, source_target_pairs={{0,2},{1,15},{2,0},{3,5},{4,6},{5,3},{6,4},{7,9},{8,10},{9,7},{10,... | collective-permute-start | bytes 884744 | tf_op jit(solution)/shard_map/ppermute | solution.py:161
  109.5 7.9 %collective-permute-start.11 = (bf16[144,256]{1,0:T(8,128)(2,1)S(1)}, bf16[144,256]{1,0:T(8,128)(2,1)S(1)}, u32[]{:S(2)}, u32[]{:S(2)}) collective-permute-start(bf16[144,256]{1,0:T(8,128)(2,1)S(1)} %get-tuple-element.255), channel_id=1, source_target_pairs={{0,8},{1,9},{2,10},{3,11},{4,12},{5,13},{6,14},{7,15},{8,0},{9,1},... | collective-permute-start | bytes 221192 | tf_op jit(solution)/shard_map/ppermute | solution.py:169
  113.8 7.0 %collective-permute-start.12 = (bf16[144,256]{1,0:T(8,128)(2,1)S(1)}, bf16[144,256]{1,0:T(8,128)(2,1)S(1)}, u32[]{:S(2)}, u32[]{:S(2)}) collective-permute-start(bf16[144,256]{1,0:T(8,128)(2,1)S(1)} %get-tuple-element.256), channel_id=1, source_target_pairs={{0,4},{1,5},{2,6},{3,7},{4,8},{5,9},{6,10},{7,11},{8,12},{9,13},{1... | collective-permute-start | bytes 221192 | tf_op jit(solution)/shard_map/ppermute | solution.py:169
  113.8 8.9 %collective-permute-start.13 = (bf16[144,256]{1,0:T(8,128)(2,1)S(1)}, bf16[144,256]{1,0:T(8,128)(2,1)S(1)}, u32[]{:S(2)}, u32[]{:S(2)}) collective-permute-start(bf16[144,256]{1,0:T(8,128)(2,1)S(1)} %get-tuple-element.257), channel_id=1, source_target_pairs={{0,12},{1,13},{2,14},{3,15},{4,0},{5,1},{6,2},{7,3},{8,4},{9,5},{1... | collective-permute-start | bytes 221192 | tf_op jit(solution)/shard_map/ppermute | solution.py:169
